TPU v7x, 256 devices: a whole 4x4x8 slice. The times are simulated.
256 devices in a mesh: dp: 2 (over core), lon: 16 (over x, y), lat: 8 (over z).
Axes of the slice: x: 4, y: 4, z: 8, core: 2. Of those that a mesh axis runs over, the one named last changes fastest.
Arguments:
- obs_values: bfloat16 [2, 16, 8, 64, 16, 512], P('dp', 'lon', 'lat'), may hold values from -6 to 6
- obs_coords: float32 [2, 16, 8, 64, 2, 512], P('dp', 'lon', 'lat'), may hold values from -0.5 to 15.5
- obs_dest: int32 [2, 16, 8, 64], P('dp', 'lon', 'lat'), may hold values from 0 to 127, as said below
- obs_count: int32 [2, 16, 8, 64], P('dp', 'lon', 'lat'), may hold values from 1 to 512
- embed_weight: bfloat16 [17, 256], replicated, may hold values from -1.5 to 1.5
- patch_weight: bfloat16 [1024, 256], replicated, may hold values from -0.1875 to 0.1875
- depth_kernel: bfloat16 [2, 49, 256], replicated, may hold values from -0.875 to 0.875
- expand_weight: bfloat16 [2, 256, 1024], replicated, may hold values from -0.375 to 0.375
- reduce_weight: bfloat16 [2, 1024, 256], replicated, may hold values from -0.1875 to 0.1875
- out_cotangent: bfloat16 [2, 128, 64, 256], P('dp', 'lon', 'lat'), may hold values from -0.125 to 0.125
Outputs:
- features: bfloat16 [2, 128, 64, 256], P('dp', 'lon', 'lat')
- grad_embed: float32 [17, 256], replicated
- grad_patch: float32 [1024, 256], replicated
- grad_kernel: float32 [2, 49, 256], replicated
- grad_expand: float32 [2, 256, 1024], replicated
- grad_reduce: float32 [2, 1024, 256], replicated
Inputs may be any that keep to these rules, and one draw needn't show every extreme that they name: `obs_dest`: the 64 ids of one device are distinct; in every window some tile is named by every device of that window.
All inputs are finite; a program needn't handle non-finite values.
Results may differ from a plain program's by a relative error of at most 0.02.
Values may be sent and summed in bfloat16 or wider, within the bound.
A program may use at most 64 MiB of HBM per device.

v0:
```python
import math

import jax
import jax.numpy as jnp
from jax import lax
from jax.sharding import PartitionSpec as P

OBSF = 16
KSIDE = 7
BLOCKS = 2
TILE = 16


LENGTH_SCALE = 0.7


def padded_2(array, sides, width):
    for axis, dim in sides:
        peers, length = (lax.axis_size(axis), array.shape[dim])
        up = [(i, (i + 1) % peers) for i in range(peers)]
        down = [(j, i) for i, j in up]
        last = lax.slice_in_dim(array, length - width, length, axis=dim)
        leading = lax.slice_in_dim(array, 0, width, axis=dim)
        before = lax.ppermute(last, axis, up)
        after = lax.ppermute(leading, axis, down)
        array = jnp.concatenate([before, array, after], axis=dim)
    return array


def layer_norm(field):
    center = jnp.mean(field, axis=-1, keepdims=True)
    spread = jnp.mean(jnp.square(field - center), axis=-1, keepdims=True)
    return (field - center) * lax.rsqrt(spread + 1e-05)


def exact_gelu(field):
    return jax.nn.gelu(field, approximate=False)


def encode_group(block_values, block_coords, row_counts, tile_side):
    chan_len = block_values.shape[1]
    row_len = block_values.shape[2]
    positions = jnp.arange(row_len, dtype=jnp.int32)
    live = (
        (positions[None, :] < row_counts[:, None].astype(jnp.int32)).astype(jnp.float32).reshape(-1)
    )
    cells = jnp.arange(tile_side).astype(jnp.float32)
    inverse = 0.5 / (LENGTH_SCALE * LENGTH_SCALE)
    lon_pos = block_coords[:, 0, :].reshape(-1)
    lat_pos = block_coords[:, 1, :].reshape(-1)
    lon_factor = jnp.exp(-jnp.square(lon_pos[None, :] - cells[:, None]) * inverse) * live[None, :]
    lat_factor = jnp.exp(-jnp.square(lat_pos[None, :] - cells[:, None]) * inverse).astype(
        jnp.bfloat16
    )
    data = jnp.transpose(block_values, (1, 0, 2)).reshape(chan_len, -1).astype(jnp.float32)
    data = jnp.concatenate([data, jnp.ones((1, data.shape[1]), jnp.float32)], axis=0)
    weighted = (data[:, None, :] * lon_factor[None, :, :]).astype(jnp.bfloat16)
    flat = weighted.reshape((chan_len + 1) * tile_side, -1)
    product = lax.dot_general(
        lat_factor, flat, (((1,), (1,)), ((), ())), preferred_element_type=jnp.float32
    )
    product = product.reshape(tile_side, chan_len + 1, tile_side)
    return jnp.transpose(product, (1, 2, 0))


def finish_tile(sums):
    density = sums[-1]
    scaled = sums[:-1] * lax.rsqrt(1.0 + density)[None]
    channels = jnp.concatenate([scaled, 0.25 * jnp.log1p(density)[None]], axis=0)
    return jnp.transpose(channels, (1, 2, 0)).astype(jnp.bfloat16)


def to_patches(field):
    batch_len, lon_len, lat_len, chan_len = field.shape
    grouped = field.reshape(batch_len, lon_len // 2, 2, lat_len // 2, 2, chan_len)
    grouped = jnp.transpose(grouped, (0, 1, 3, 2, 4, 5))
    return grouped.reshape(batch_len * (lon_len // 2) * (lat_len // 2), 4 * chan_len)


def from_patches(flat, batch_len, lon_len, lat_len, chan_len):
    grouped = flat.reshape(batch_len, lon_len // 2, lat_len // 2, 2, 2, chan_len)
    grouped = jnp.transpose(grouped, (0, 1, 3, 2, 4, 5))
    return grouped.reshape(batch_len, lon_len, lat_len, chan_len)


def depthwise(padded, kernel):
    kernel_side = int(math.isqrt(kernel.shape[0]))
    lon_len = padded.shape[1] - kernel_side + 1
    lat_len = padded.shape[2] - kernel_side + 1
    running = jnp.zeros((padded.shape[0], lon_len, lat_len, padded.shape[3]), jnp.float32)
    for tap_row in range(kernel_side):
        for tap_col in range(kernel_side):
            running = (
                running
                + padded[:, tap_row : tap_row + lon_len, tap_col : tap_col + lat_len, :]
                * kernel[tap_row * kernel_side + tap_col]
            )
    return running


def kernel_grad(padded, grad_out):
    kernel_side = padded.shape[1] - grad_out.shape[1] + 1
    lon_len = grad_out.shape[1]
    lat_len = grad_out.shape[2]
    taps = []
    for tap_row in range(kernel_side):
        for tap_col in range(kernel_side):
            piece = padded[:, tap_row : tap_row + lon_len, tap_col : tap_col + lat_len, :]
            taps.append(jnp.sum(piece * grad_out, axis=(0, 1, 2)))
    return jnp.stack(taps)


def input_grad(grad_padded, kernel):
    kernel_side = int(math.isqrt(kernel.shape[0]))
    lon_len = grad_padded.shape[1] - kernel_side + 1
    lat_len = grad_padded.shape[2] - kernel_side + 1
    twice = 2 * (kernel_side // 2)
    running = jnp.zeros((grad_padded.shape[0], lon_len, lat_len, grad_padded.shape[3]), jnp.float32)
    for tap_row in range(kernel_side):
        for tap_col in range(kernel_side):
            row_start = twice - tap_row
            col_start = twice - tap_col
            running = (
                running
                + grad_padded[
                    :, row_start : row_start + lon_len, col_start : col_start + lat_len, :
                ]
                * kernel[tap_row * kernel_side + tap_col]
            )
    return running


def stem_forward(encoded, embed_weight, patch_weight):
    batch_len, lon_len, lat_len, chan_in = encoded.shape
    embedded = jnp.dot(
        encoded.reshape(-1, chan_in), embed_weight, preferred_element_type=jnp.float32
    )
    embedded = embedded.reshape(batch_len, lon_len, lat_len, -1)
    normed_grid = layer_norm(embedded).astype(jnp.bfloat16)
    first = jnp.dot(
        to_patches(normed_grid), patch_weight, preferred_element_type=jnp.float32
    ).astype(jnp.bfloat16)
    first = first.reshape(batch_len, lon_len // 2, lat_len // 2, -1)
    return (embedded, normed_grid, first)


def block_forward(state, padded, kernel, expand, reduce_weight):
    chan_len = state.shape[3]
    depth_out = depthwise(padded.astype(jnp.float32), kernel.astype(jnp.float32))
    normed = layer_norm(depth_out).astype(jnp.bfloat16)
    act = jnp.dot(normed.reshape(-1, chan_len), expand, preferred_element_type=jnp.float32)
    hidden = exact_gelu(act).astype(jnp.bfloat16)
    branch = jnp.dot(hidden, reduce_weight, preferred_element_type=jnp.float32).reshape(state.shape)
    following = (state.astype(jnp.float32) + branch).astype(jnp.bfloat16)
    return (following, (depth_out, normed, act, hidden))


def block_backward(grad_next, padded, stored, kernel, expand, reduce_weight, extend):
    depth_out, normed, act, hidden = stored
    chan_len = grad_next.shape[3]
    grad_flat = grad_next.reshape(-1, chan_len)
    g_reduce = jnp.dot(hidden.T, grad_flat, preferred_element_type=jnp.float32)
    grad_hidden = jnp.dot(grad_flat, reduce_weight.T, preferred_element_type=jnp.float32)
    grad_act = jax.vjp(exact_gelu, act)[1](grad_hidden)[0].astype(jnp.bfloat16)
    g_expand = jnp.dot(normed.reshape(-1, chan_len).T, grad_act, preferred_element_type=jnp.float32)
    grad_normed = jnp.dot(grad_act, expand.T, preferred_element_type=jnp.float32).reshape(
        grad_next.shape
    )
    grad_depth = jax.vjp(layer_norm, depth_out)[1](grad_normed)[0]
    g_kernel = kernel_grad(padded.astype(jnp.float32), grad_depth)
    grad_state = grad_next.astype(jnp.float32) + input_grad(
        extend(grad_depth), kernel.astype(jnp.float32)
    )
    return (grad_state.astype(jnp.bfloat16), g_kernel, g_expand, g_reduce)


def stem_backward(grad_first, encoded, embedded, normed_grid, patch_weight):
    batch_len, lon_len, lat_len, chan_in = encoded.shape
    chan_len = grad_first.shape[3]
    grad_flat = grad_first.reshape(-1, chan_len)
    g_patch = jnp.dot(to_patches(normed_grid).T, grad_flat, preferred_element_type=jnp.float32)
    grad_normed = jnp.dot(grad_flat, patch_weight.T, preferred_element_type=jnp.float32)
    grad_normed = from_patches(grad_normed, batch_len, lon_len, lat_len, chan_len)
    grad_embedded = jax.vjp(layer_norm, embedded)[1](grad_normed)[0].astype(jnp.bfloat16)
    g_embed = jnp.dot(
        encoded.reshape(-1, chan_in).T,
        grad_embedded.reshape(-1, chan_len),
        preferred_element_type=jnp.float32,
    )
    return (g_embed, g_patch)


def lat_edges(grown):
    reach = KSIDE // 2
    lat_index = lax.axis_index("lat")
    lat_count = lax.axis_size("lat")
    columns = jnp.arange(grown.shape[1])
    keep = ((columns >= reach) | (lat_index > 0)) & (
        (columns < grown.shape[1] - reach) | (lat_index < lat_count - 1)
    )
    return grown * keep[None, :, None].astype(grown.dtype)


def extend_grid(field):
    grown = padded_2(field[0], (("lon", 0), ("lat", 1)), KSIDE // 2)
    return lat_edges(grown)[None]


def extend_grad(field):
    grown = padded_2(field[0].astype(jnp.bfloat16), (("lon", 0), ("lat", 1)), KSIDE // 2).astype(
        jnp.float32
    )
    return lat_edges(grown)[None]


def on_device(
    obs_values,
    obs_coords,
    obs_dest,
    obs_count,
    embed_weight,
    patch_weight,
    depth_kernel,
    expand_weight,
    reduce_weight,
    out_cotangent,
):
    block_values = obs_values[0, 0, 0]
    block_coords = obs_coords[0, 0, 0]
    dest_tiles = obs_dest[0, 0, 0]
    row_counts = obs_count[0, 0, 0]
    lon_count = lax.axis_size("lon")
    lat_count = lax.axis_size("lat")
    tile_count = lon_count * lat_count
    send_values = (
        jnp.zeros((tile_count,) + block_values.shape[1:], block_values.dtype)
        .at[dest_tiles]
        .set(block_values)
    )
    send_coords = (
        jnp.zeros((tile_count,) + block_coords.shape[1:], jnp.float32)
        .at[dest_tiles]
        .set(block_coords)
    )
    send_counts = jnp.zeros((tile_count,), jnp.int32).at[dest_tiles].set(row_counts)
    got_values, got_coords, got_counts = (
        lax.all_to_all(
            send_values.astype(jnp.float32), ("lon", "lat"), split_axis=0, concat_axis=0, tiled=True
        ).astype(send_values.dtype),
        lax.all_to_all(send_coords, ("lon", "lat"), split_axis=0, concat_axis=0, tiled=True),
        lax.all_to_all(send_counts, ("lon", "lat"), split_axis=0, concat_axis=0, tiled=True),
    )
    slot_group = 8
    empty_sums = jnp.zeros((OBSF + 1, TILE, TILE), jnp.float32)
    group_count = tile_count // slot_group
    grouped = (
        got_values.reshape((group_count, slot_group) + got_values.shape[1:]),
        got_coords.reshape((group_count, slot_group) + got_coords.shape[1:]),
        got_counts.reshape(group_count, slot_group),
    )

    def scan_group(running, pieces):
        return (running + encode_group(pieces[0], pieces[1], pieces[2], TILE), None)

    sums, unused = lax.scan(scan_group, empty_sums, grouped)
    encoded = finish_tile(sums)[None]
    embedded, normed_grid, state = stem_forward(encoded, embed_weight, patch_weight)
    records = []
    for index in range(BLOCKS):
        padded = extend_grid(state)
        following, stored = block_forward(
            state, padded, depth_kernel[index], expand_weight[index], reduce_weight[index]
        )
        records.append((padded, stored))
        state = following
    cotangent = out_cotangent
    kernels = [None] * BLOCKS
    expands = [None] * BLOCKS
    reduces = [None] * BLOCKS
    for index in reversed(range(BLOCKS)):
        padded, stored = records[index]
        cotangent, g_kernel, g_expand, g_reduce = block_backward(
            cotangent,
            padded,
            stored,
            depth_kernel[index],
            expand_weight[index],
            reduce_weight[index],
            extend_grad,
        )
        kernels[index] = g_kernel
        expands[index] = g_expand
        reduces[index] = g_reduce
    g_embed, g_patch = stem_backward(cotangent, encoded, embedded, normed_grid, patch_weight)
    grad_kernel = jnp.stack(kernels)
    grad_expand = jnp.stack(expands)
    grad_reduce = jnp.stack(reduces)
    g_embed, g_patch, grad_kernel, grad_expand, grad_reduce = lax.psum(
        (g_embed, g_patch, grad_kernel, grad_expand, grad_reduce), ("dp", "lon", "lat")
    )
    return (state, g_embed, g_patch, grad_kernel, grad_expand, grad_reduce)


def solution(mesh):
    in_specs = (
        P("dp", "lon", "lat", None, None, None),
        P("dp", "lon", "lat", None, None, None),
        P("dp", "lon", "lat", None),
        P("dp", "lon", "lat", None),
        P(),
        P(),
        P(),
        P(),
        P(),
        P("dp", "lon", "lat", None),
    )
    out_specs = (P("dp", "lon", "lat", None), P(), P(), P(), P(), P())
    return jax.shard_map(
        on_device, mesh=mesh, in_specs=in_specs, out_specs=out_specs, check_vma=False
    )
```

profile of v0, /device:TPU:1, one launch (start us, length us, event | category | flops | bytes accessed | tf_op | source)
XLA Modules:
  0.0 516.0 jit_solution(4185064165762549314)
XLA Ops:
  7.9 0.9 scatter_custom_fusion.2
  9.5 16.3 %all-to-all-start.2 = ((s32[128,1,1]{2,1,0:T(1,128)}), s32[128,1,1]{2,1,0:T(1,128)S(1)}, u32[]{:S(2)}, u32[]{:S(2)}) async-start(s32[128,1,1]{2,1,0:T(1,128)} %copy.33), calls=%async_computation.2 | async-start | bytes 131072 | tf_op jit(solution)/shard_map/all_to_all | solution.py:251
  25.9 0.9 broadcast_in_dim.22
  26.8 7.5 %scatter_fusion.1 = f32[128,2,512]{2,1,0:T(2,128)} fusion(f32[128,2,512]{2,1,0:T(2,128)} %broadcast_in_dim.22, s32[64]{0:T(128)S(1)} %fusion.179, f32[64,2,512]{2,1,0:T(2,128)} %bitcast.434), kind=kCustom, calls=%fused_computation.1 | custom fusion | bytes 786688 | tf_op jit(solution)/shard_map/scatter | solution.py:243
  34.3 2.1 all-to-all-done.2
  36.4 11.2 %all-to-all-start.1 = ((f32[128,2,512]{2,1,0:T(2,128)}), f32[128,2,512]{2,1,0:T(2,128)S(1)}, u32[]{:S(2)}, u32[]{:S(2)}) async-start(f32[128,2,512]{2,1,0:T(2,128)} %scatter_fusion.1), calls=%async_computation.1 | async-start | bytes 1048576 | tf_op jit(solution)/shard_map/all_to_all | solution.py:250
  47.6 1.6 broadcast_in_dim.21
  49.1 8.1 %scatter_fusion = bf16[128,16,512]{2,1,0:T(8,128)(2,1)} fusion(bf16[128,16,512]{2,1,0:T(8,128)(2,1)} %broadcast_in_dim.21, s32[64]{0:T(128)S(1)} %fusion.179, bf16[64,16,512]{2,1,0:T(8,128)(2,1)S(1)} %bitcast.429), kind=kCustom, calls=%fused_computation | custom fusion | bytes 3145984 | tf_op jit(solution)/shard_map/scatter | solution.py:238
  57.3 9.0 %all-to-all-done.1 = f32[128,2,512]{2,1,0:T(2,128)S(1)} async-done(((f32[128,2,512]{2,1,0:T(2,128)}), f32[128,2,512]{2,1,0:T(2,128)S(1)}, u32[]{:S(2)}, u32[]{:S(2)}) %all-to-all-start.1) | async-done | bytes 524320 | tf_op jit(solution)/shard_map/all_to_all | solution.py:250
  66.2 6.5 %all-to-all-start = ((bf16[128,16,512]{2,1,0:T(8,128)(2,1)}), bf16[128,16,512]{2,1,0:T(8,128)(2,1)S(1)}, u32[]{:S(2)}, u32[]{:S(2)}) async-start(bf16[128,16,512]{2,1,0:T(8,128)(2,1)} %scatter_fusion), calls=%async_computation | async-start | bytes 4194304 | tf_op jit(solution)/shard_map/all_to_all | solution.py:247
  75.6 2.3 reduce.18
  78.0 45.4 %all-to-all-done = bf16[128,16,512]{2,1,0:T(8,128)(2,1)S(1)} async-done(((bf16[128,16,512]{2,1,0:T(8,128)(2,1)}), bf16[128,16,512]{2,1,0:T(8,128)(2,1)S(1)}, u32[]{:S(2)}, u32[]{:S(2)}) %all-to-all-start) | async-done | bytes 2097184 | tf_op jit(solution)/shard_map/all_to_all | solution.py:247
  123.4 19.2 %while.11 = (s32[]{:T(128)}, f32[17,16,16]{2,1,0:T(8,128)S(1)}, bf16[16,8,16,512]{3,2,1,0:T(8,128)(2,1)S(1)}, f32[16,8,2,512]{3,2,1,0:T(2,128)S(1)}, s32[16,8]{1,0:T(8,128)S(1)}, /*index=5*/s32[]{:T(128)}, s32[]{:T(128)}) while((s32[]{:T(128)}, f32[17,16,16]{2,1,0:T(8,128)S(1)}, bf16[16,8,16,512]{3,2,1,0:T(8,128)(2,1)S(1)}, ...), condition=%wide.region_4.5_spmd.clone, body=%wide.region_3.4_spmd.clone.sunk | while | flops 38621712 | bytes 2001291 | solution.py:265
  123.8 0.8 fusion.229
  125.0 0.8 fusion.229
  126.2 0.8 fusion.229
  127.4 0.8 fusion.229
  129.8 0.8 fusion.229
  131.0 0.8 fusion.229
  132.2 0.8 fusion.229
  133.4 0.8 fusion.229
  134.6 0.8 fusion.229
  135.8 0.8 fusion.229
  137.0 0.8 fusion.229
  138.2 0.8 fusion.229
  139.4 0.8 fusion.229
  140.7 0.8 fusion.229
  141.9 0.8 fusion.229
  146.0 4.8 collective-permute-start.1
  150.9 1.0 collective-permute-done
  151.9 1.1 collective-permute-start.2
  153.1 1.6 collective-permute-start.3
  154.7 1.5 collective-permute-done.2
  157.9 2.6 multiply_convert_fusion.5
  160.8 4.8 collective-permute-start.5
  165.7 1.0 collective-permute-done.4
  166.8 2.7 collective-permute-start.7
  172.1 2.6 multiply_convert_fusion.4
  175.8 0.9 multiply_reduce_fusion.4
  178.2 4.8 collective-permute-start.9
  185.3 2.7 collective-permute-start.11
  188.4 5.1 stack.427
  193.5 0.9 convert_multiply_fusion.1
  194.4 1.6 fusion.109
  196.0 1.3 convolution_bitcast_fusion.1
  197.6 1.4 convolution_bitcast_fusion.3
  199.8 0.9 multiply_reduce_fusion.53
  201.5 4.9 collective-permute-start.13
  206.3 1.5 pad_maximum_fusion
  207.9 1.5 pad_maximum_fusion.1
  209.8 4.3 stack.376
  214.3 2.7 collective-permute-start.15
  217.6 0.9 collective-permute-done.14
  219.6 1.2 fusion.59
  220.8 1.3 fusion.166
  222.2 1.2 copy-done.8
  223.4 0.8 fusion.13
  226.2 85.8 %psum.35 = f32[17,256]{1,0:T(8,128)} all-reduce(f32[17,256]{1,0:T(8,128)S(1)} %fusion.54), channel_id=1, replica_groups=mesh['dp'=2,'lon'=16,'lat'=8] {'dp','lon','lat'}, use_global_device_ids=true, to_apply=%region_20.21 | all-reduce | flops 4352 | bytes 34816 | tf_op jit(solution)/shard_map/psum | solution.py:298
  312.0 189.5 %all-reduce.4.cloned.1.call-done = (f32[1024,256]{1,0:T(8,128)}, f32[2,49,256]{2,1,0:T(8,128)}, f32[2,256,1024]{2,1,0:T(8,128)}, f32[2,1024,256]{2,1,0:T(8,128)}) async-done(((f32[1024,256]{1,0:T(8,128)}, f32[2,49,256]{2,1,0:T(8,128)}, f32[2,256,1024]{2,1,0:T(8,128)}, f32[2,1024,256]{2,1,0:T(8,128)}), (f32[1024,256]{1,0:T(8,128)}, f32[2,49,256]{2,1,0:T(8,128)}, f32[2,256,1024]{2,1,0:T(8,128)}, ...) | async-done | bytes 5343248 | tf_op jit(solution)/shard_map/psum | solution.py:298
  501.5 1.7 copy.42
  503.2 2.3 copy.70
  505.5 1.3 copy.71
  506.8 1.0 copy-done.3
  507.8 1.3 copy.72
  (613 shorter events, 27.8 us)
Async XLA Ops:
  7.2 138.4 %copy-start = (bf16[1024,256]{1,0:T(8,128)(2,1)S(1)}, bf16[1024,256]{1,0:T(8,128)(2,1)}, u32[]{:S(2)}) copy-start(bf16[1024,256]{1,0:T(8,128)(2,1)} %param.17) | copy-start | bytes 1572868
  9.5 26.8 %all-to-all-start.2 = ((s32[128,1,1]{2,1,0:T(1,128)}), s32[128,1,1]{2,1,0:T(1,128)S(1)}, u32[]{:S(2)}, u32[]{:S(2)}) async-start(s32[128,1,1]{2,1,0:T(1,128)} %copy.33), calls=%async_computation.2 | async-start | bytes 131072 | tf_op jit(solution)/shard_map/all_to_all | solution.py:251
  26.8 22.3 %copy-start.5 = (bf16[1,1,1,64,16,512]{5,4,3,2,1,0:T(8,128)(2,1)S(1)}, bf16[1,1,1,64,16,512]{5,4,3,2,1,0:T(8,128)(2,1)}, u32[]{:S(2)}) copy-start(bf16[1,1,1,64,16,512]{5,4,3,2,1,0:T(8,128)(2,1)} %param.12) | copy-start | bytes 3145732
  36.4 29.9 %all-to-all-start.1 = ((f32[128,2,512]{2,1,0:T(2,128)}), f32[128,2,512]{2,1,0:T(2,128)S(1)}, u32[]{:S(2)}, u32[]{:S(2)}) async-start(f32[128,2,512]{2,1,0:T(2,128)} %scatter_fusion.1), calls=%async_computation.1 | async-start | bytes 1048576 | tf_op jit(solution)/shard_map/all_to_all | solution.py:250
  57.3 15.5 %copy-start.17 = (bf16[2,49,256]{2,0,1:T(2,128)(2,1)S(1)}, bf16[2,49,256]{2,0,1:T(2,128)(2,1)}, u32[]{:S(2)}) copy-start(bf16[2,49,256]{2,0,1:T(2,128)(2,1)} %param.18) | copy-start | bytes 150532
  66.2 57.2 %all-to-all-start = ((bf16[128,16,512]{2,1,0:T(8,128)(2,1)}), bf16[128,16,512]{2,1,0:T(8,128)(2,1)S(1)}, u32[]{:S(2)}, u32[]{:S(2)}) async-start(bf16[128,16,512]{2,1,0:T(8,128)(2,1)} %scatter_fusion), calls=%async_computation | async-start | bytes 4194304 | tf_op jit(solution)/shard_map/all_to_all | solution.py:247
  72.7 428.7 %all-reduce.4.cloned.1.call-start = ((), (), s32[]{:S(2)}) async-start(), calls=%async_computation.3 | async-start | bytes 10715136 | tf_op jit(solution)/shard_map/psum | solution.py:298
  73.5 82.9 %copy-start.26 = (f32[1,1,256]{2,0,1:T(1,128)}, f32[1,1,256]{2,0,1:T(1,128)S(1)}, u32[]{:S(2)}) copy-start(f32[1,1,256]{2,0,1:T(1,128)S(1)} %get-tuple-element.299) | copy-start | bytes 3076
  73.5 82.9 %copy-start.28 = (f32[1,1,256]{2,0,1:T(1,128)}, f32[1,1,256]{2,0,1:T(1,128)S(1)}, u32[]{:S(2)}) copy-start(f32[1,1,256]{2,0,1:T(1,128)S(1)} %get-tuple-element.300) | copy-start | bytes 3076
  73.5 82.9 %copy-start.30 = (f32[1,1,256]{2,0,1:T(1,128)}, f32[1,1,256]{2,0,1:T(1,128)S(1)}, u32[]{:S(2)}) copy-start(f32[1,1,256]{2,0,1:T(1,128)S(1)} %get-tuple-element.301) | copy-start | bytes 3076
  73.5 82.9 %copy-start.32 = (f32[1,1,256]{2,0,1:T(1,128)}, f32[1,1,256]{2,0,1:T(1,128)S(1)}, u32[]{:S(2)}) copy-start(f32[1,1,256]{2,0,1:T(1,128)S(1)} %get-tuple-element.302) | copy-start | bytes 3076
  73.5 82.9 %copy-start.34 = (f32[1,1,256]{2,0,1:T(1,128)}, f32[1,1,256]{2,0,1:T(1,128)S(1)}, u32[]{:S(2)}) copy-start(f32[1,1,256]{2,0,1:T(1,128)S(1)} %get-tuple-element.303) | copy-start | bytes 3076
  73.5 82.9 %copy-start.36 = (f32[1,1,256]{2,0,1:T(1,128)}, f32[1,1,256]{2,0,1:T(1,128)S(1)}, u32[]{:S(2)}) copy-start(f32[1,1,256]{2,0,1:T(1,128)S(1)} %get-tuple-element.304) | copy-start | bytes 3076
  73.5 82.9 %copy-start.38 = (f32[1,1,256]{2,0,1:T(1,128)}, f32[1,1,256]{2,0,1:T(1,128)S(1)}, u32[]{:S(2)}) copy-start(f32[1,1,256]{2,0,1:T(1,128)S(1)} %get-tuple-element.305) | copy-start | bytes 3076
  73.5 82.9 %copy-start.40 = (f32[1,1,256]{2,0,1:T(1,128)}, f32[1,1,256]{2,0,1:T(1,128)S(1)}, u32[]{:S(2)}) copy-start(f32[1,1,256]{2,0,1:T(1,128)S(1)} %get-tuple-element.306) | copy-start | bytes 3076
  73.5 82.9 %copy-start.42 = (f32[1,1,256]{2,0,1:T(1,128)}, f32[1,1,256]{2,0,1:T(1,128)S(1)}, u32[]{:S(2)}) copy-start(f32[1,1,256]{2,0,1:T(1,128)S(1)} %get-tuple-element.307) | copy-start | bytes 3076
  73.5 82.9 %copy-start.44 = (f32[1,1,256]{2,0,1:T(1,128)}, f32[1,1,256]{2,0,1:T(1,128)S(1)}, u32[]{:S(2)}) copy-start(f32[1,1,256]{2,0,1:T(1,128)S(1)} %get-tuple-element.308) | copy-start | bytes 3076
  73.5 82.9 %copy-start.46 = (f32[1,1,256]{2,0,1:T(1,128)}, f32[1,1,256]{2,0,1:T(1,128)S(1)}, u32[]{:S(2)}) copy-start(f32[1,1,256]{2,0,1:T(1,128)S(1)} %get-tuple-element.309) | copy-start | bytes 3076
  73.6 82.9 %copy-start.48 = (f32[1,1,256]{2,0,1:T(1,128)}, f32[1,1,256]{2,0,1:T(1,128)S(1)}, u32[]{:S(2)}) copy-start(f32[1,1,256]{2,0,1:T(1,128)S(1)} %get-tuple-element.310) | copy-start | bytes 3076
  73.6 82.9 %copy-start.50 = (f32[1,1,256]{2,0,1:T(1,128)}, f32[1,1,256]{2,0,1:T(1,128)S(1)}, u32[]{:S(2)}) copy-start(f32[1,1,256]{2,0,1:T(1,128)S(1)} %get-tuple-element.311) | copy-start | bytes 3076
  73.6 82.9 %copy-start.52 = (f32[1,1,256]{2,0,1:T(1,128)}, f32[1,1,256]{2,0,1:T(1,128)S(1)}, u32[]{:S(2)}) copy-start(f32[1,1,256]{2,0,1:T(1,128)S(1)} %get-tuple-element.312) | copy-start | bytes 3076
  73.6 82.9 %copy-start.54 = (f32[1,1,256]{2,0,1:T(1,128)}, f32[1,1,256]{2,0,1:T(1,128)S(1)}, u32[]{:S(2)}) copy-start(f32[1,1,256]{2,0,1:T(1,128)S(1)} %get-tuple-element.313) | copy-start | bytes 3076
  73.6 82.9 %copy-start.56 = (f32[1,1,256]{2,0,1:T(1,128)}, f32[1,1,256]{2,0,1:T(1,128)S(1)}, u32[]{:S(2)}) copy-start(f32[1,1,256]{2,0,1:T(1,128)S(1)} %get-tuple-element.314) | copy-start | bytes 3076
  73.6 82.9 %copy-start.58 = (f32[1,1,256]{2,0,1:T(1,128)}, f32[1,1,256]{2,0,1:T(1,128)S(1)}, u32[]{:S(2)}) copy-start(f32[1,1,256]{2,0,1:T(1,128)S(1)} %get-tuple-element.315) | copy-start | bytes 3076
  73.6 82.9 %copy-start.60 = (f32[1,1,256]{2,0,1:T(1,128)}, f32[1,1,256]{2,0,1:T(1,128)S(1)}, u32[]{:S(2)}) copy-start(f32[1,1,256]{2,0,1:T(1,128)S(1)} %get-tuple-element.316) | copy-start | bytes 3076
  123.4 19.6 %copy-start.25 = (bf16[17,256]{1,0:T(8,128)(2,1)S(1)}, bf16[17,256]{1,0:T(8,128)(2,1)}, u32[]{:S(2)}) copy-start(bf16[17,256]{1,0:T(8,128)(2,1)} %param.16) | copy-start | bytes 26116
  142.7 13.8 %copy-start.62 = (f32[1,1,256]{2,0,1:T(1,128)S(1)}, f32[1,1,256]{2,0,1:T(1,128)}, u32[]{:S(2)}) copy-start(f32[1,1,256]{2,0,1:T(1,128)} %get-tuple-element.317) | copy-start | bytes 3076
  142.7 13.8 %copy-start.64 = (f32[1,1,256]{2,0,1:T(1,128)S(1)}, f32[1,1,256]{2,0,1:T(1,128)}, u32[]{:S(2)}) copy-start(f32[1,1,256]{2,0,1:T(1,128)} %get-tuple-element.280) | copy-start | bytes 3076
  142.7 13.8 %copy-start.66 = (f32[1,1,256]{2,0,1:T(1,128)S(1)}, f32[1,1,256]{2,0,1:T(1,128)}, u32[]{:S(2)}) copy-start(f32[1,1,256]{2,0,1:T(1,128)} %get-tuple-element.281) | copy-start | bytes 3076
  142.7 13.8 %copy-start.68 = (f32[1,1,256]{2,0,1:T(1,128)S(1)}, f32[1,1,256]{2,0,1:T(1,128)}, u32[]{:S(2)}) copy-start(f32[1,1,256]{2,0,1:T(1,128)} %get-tuple-element.282) | copy-start | bytes 3076
  142.7 13.8 %copy-start.70 = (f32[1,1,256]{2,0,1:T(1,128)S(1)}, f32[1,1,256]{2,0,1:T(1,128)}, u32[]{:S(2)}) copy-start(f32[1,1,256]{2,0,1:T(1,128)} %get-tuple-element.283) | copy-start | bytes 3076
  142.7 13.8 %copy-start.72 = (f32[1,1,256]{2,0,1:T(1,128)S(1)}, f32[1,1,256]{2,0,1:T(1,128)}, u32[]{:S(2)}) copy-start(f32[1,1,256]{2,0,1:T(1,128)} %get-tuple-element.284) | copy-start | bytes 3076
  142.8 13.8 %copy-start.74 = (f32[1,1,256]{2,0,1:T(1,128)S(1)}, f32[1,1,256]{2,0,1:T(1,128)}, u32[]{:S(2)}) copy-start(f32[1,1,256]{2,0,1:T(1,128)} %get-tuple-element.285) | copy-start | bytes 3076
  142.8 13.8 %copy-start.76 = (f32[1,1,256]{2,0,1:T(1,128)S(1)}, f32[1,1,256]{2,0,1:T(1,128)}, u32[]{:S(2)}) copy-start(f32[1,1,256]{2,0,1:T(1,128)} %get-tuple-element.286) | copy-start | bytes 3076
  142.8 13.8 %copy-start.78 = (f32[1,1,256]{2,0,1:T(1,128)S(1)}, f32[1,1,256]{2,0,1:T(1,128)}, u32[]{:S(2)}) copy-start(f32[1,1,256]{2,0,1:T(1,128)} %get-tuple-element.287) | copy-start | bytes 3076
  142.8 13.8 %copy-start.80 = (f32[1,1,256]{2,0,1:T(1,128)S(1)}, f32[1,1,256]{2,0,1:T(1,128)}, u32[]{:S(2)}) copy-start(f32[1,1,256]{2,0,1:T(1,128)} %get-tuple-element.288) | copy-start | bytes 3076
  142.8 13.8 %copy-start.82 = (f32[1,1,256]{2,0,1:T(1,128)S(1)}, f32[1,1,256]{2,0,1:T(1,128)}, u32[]{:S(2)}) copy-start(f32[1,1,256]{2,0,1:T(1,128)} %get-tuple-element.289) | copy-start | bytes 3076
  142.8 13.8 %copy-start.84 = (f32[1,1,256]{2,0,1:T(1,128)S(1)}, f32[1,1,256]{2,0,1:T(1,128)}, u32[]{:S(2)}) copy-start(f32[1,1,256]{2,0,1:T(1,128)} %get-tuple-element.290) | copy-start | bytes 3076
  142.8 13.8 %copy-start.86 = (f32[1,1,256]{2,0,1:T(1,128)S(1)}, f32[1,1,256]{2,0,1:T(1,128)}, u32[]{:S(2)}) copy-start(f32[1,1,256]{2,0,1:T(1,128)} %get-tuple-element.291) | copy-start | bytes 3076
  142.8 13.8 %copy-start.88 = (f32[1,1,256]{2,0,1:T(1,128)S(1)}, f32[1,1,256]{2,0,1:T(1,128)}, u32[]{:S(2)}) copy-start(f32[1,1,256]{2,0,1:T(1,128)} %get-tuple-element.292) | copy-start | bytes 3076
  142.8 13.8 %copy-start.90 = (f32[1,1,256]{2,0,1:T(1,128)S(1)}, f32[1,1,256]{2,0,1:T(1,128)}, u32[]{:S(2)}) copy-start(f32[1,1,256]{2,0,1:T(1,128)} %get-tuple-element.293) | copy-start | bytes 3076
  142.8 13.8 %copy-start.92 = (f32[1,1,256]{2,0,1:T(1,128)S(1)}, f32[1,1,256]{2,0,1:T(1,128)}, u32[]{:S(2)}) copy-start(f32[1,1,256]{2,0,1:T(1,128)} %get-tuple-element.294) | copy-start | bytes 3076
  142.9 13.8 %copy-start.94 = (f32[1,1,256]{2,0,1:T(1,128)S(1)}, f32[1,1,256]{2,0,1:T(1,128)}, u32[]{:S(2)}) copy-start(f32[1,1,256]{2,0,1:T(1,128)} %get-tuple-element.295) | copy-start | bytes 3076
  142.9 13.8 %copy-start.96 = (f32[1,1,256]{2,0,1:T(1,128)S(1)}, f32[1,1,256]{2,0,1:T(1,128)}, u32[]{:S(2)}) copy-start(f32[1,1,256]{2,0,1:T(1,128)} %get-tuple-element.296) | copy-start | bytes 3076
  142.9 13.8 %copy-start.98 = (f32[1,1,256]{2,0,1:T(1,128)S(1)}, f32[1,1,256]{2,0,1:T(1,128)}, u32[]{:S(2)}) copy-start(f32[1,1,256]{2,0,1:T(1,128)} %get-tuple-element.297) | copy-start | bytes 3076
  142.9 13.8 %copy-start.100 = (f32[1,1,256]{2,0,1:T(1,128)S(1)}, f32[1,1,256]{2,0,1:T(1,128)}, u32[]{:S(2)}) copy-start(f32[1,1,256]{2,0,1:T(1,128)} %get-tuple-element.298) | copy-start | bytes 3076
  145.8 6.1 %collective-permute-start = (bf16[3,8,256]{2,1,0:T(8,128)(2,1)S(1)}, bf16[3,8,256]{2,1,0:T(8,128)(2,1)S(1)}, u32[]{:S(2)}, u32[]{:S(2)}) collective-permute-start(bf16[3,8,256]{2,1,0:T(8,128)(2,1)S(1)} %get-tuple-element.337), channel_id=1, source_target_pairs={{0,8},{8,16},{16,24},{24,32},{32,40},{40,48},{48,56},{56,64},{64,7... | collective-permute-start | bytes 36872 | tf_op jit(solution)/shard_map/ppermute | solution.py:24
  146.0 5.9 %collective-permute-start.1 = (bf16[3,8,256]{2,1,0:T(8,128)(2,1)S(1)}, bf16[3,8,256]{2,1,0:T(8,128)(2,1)S(1)}, u32[]{:S(2)}, u32[]{:S(2)}) collective-permute-start(bf16[3,8,256]{2,1,0:T(8,128)(2,1)S(1)} %get-tuple-element.338), channel_id=1, source_target_pairs={{8,0},{16,8},{24,16},{32,24},{40,32},{48,40},{56,48},{64,56},{72,6... | collective-permute-start | bytes 36872 | tf_op jit(solution)/shard_map/ppermute | solution.py:25
  150.9 20.9 %copy-start.104 = (f32[1,1,256]{2,0,1:T(1,128)}, f32[1,1,256]{2,0,1:T(1,128)S(1)}, u32[]{:S(2)}) copy-start(f32[1,1,256]{2,0,1:T(1,128)S(1)} %get-tuple-element.319) | copy-start | bytes 3076
  150.9 20.8 %copy-start.105 = (f32[1,1,256]{2,0,1:T(1,128)}, f32[1,1,256]{2,0,1:T(1,128)S(1)}, u32[]{:S(2)}) copy-start(f32[1,1,256]{2,0,1:T(1,128)S(1)} %get-tuple-element.320) | copy-start | bytes 3076
  151.9 4.3 collective-permute-start.2
  153.1 3.2 collective-permute-start.3
  160.7 5.9 %collective-permute-start.4 = (bf16[3,8,256]{2,1,0:T(8,128)(2,1)S(1)}, bf16[3,8,256]{2,1,0:T(8,128)(2,1)S(1)}, u32[]{:S(2)}, u32[]{:S(2)}) collective-permute-start(bf16[3,8,256]{2,1,0:T(8,128)(2,1)S(1)} %get-tuple-element.335), channel_id=1, source_target_pairs={{0,8},{8,16},{16,24},{24,32},{32,40},{40,48},{48,56},{56,64},{64,7... | collective-permute-start | bytes 36872 | tf_op jit(solution)/shard_map/ppermute | solution.py:24
  160.8 5.9 %collective-permute-start.5 = (bf16[3,8,256]{2,1,0:T(8,128)(2,1)S(1)}, bf16[3,8,256]{2,1,0:T(8,128)(2,1)S(1)}, u32[]{:S(2)}, u32[]{:S(2)}) collective-permute-start(bf16[3,8,256]{2,1,0:T(8,128)(2,1)S(1)} %get-tuple-element.336), channel_id=1, source_target_pairs={{8,0},{16,8},{24,16},{32,24},{40,32},{48,40},{56,48},{64,56},{72,6... | collective-permute-start | bytes 36872 | tf_op jit(solution)/shard_map/ppermute | solution.py:25
  166.7 4.0 collective-permute-start.6
  166.8 3.9 collective-permute-start.7
  178.2 5.9 %collective-permute-start.8 = (bf16[3,8,256]{2,1,0:T(8,128)(2,1)S(1)}, bf16[3,8,256]{2,1,0:T(8,128)(2,1)S(1)}, u32[]{:S(2)}, u32[]{:S(2)}) collective-permute-start(bf16[3,8,256]{2,1,0:T(8,128)(2,1)S(1)} %get-tuple-element.333), channel_id=1, source_target_pairs={{0,8},{8,16},{16,24},{24,32},{32,40},{40,48},{48,56},{56,64},{64,7... | collective-permute-start | bytes 36872 | tf_op jit(solution)/shard_map/ppermute | solution.py:24
  178.2 5.9 %collective-permute-start.9 = (bf16[3,8,256]{2,1,0:T(8,128)(2,1)S(1)}, bf16[3,8,256]{2,1,0:T(8,128)(2,1)S(1)}, u32[]{:S(2)}, u32[]{:S(2)}) collective-permute-start(bf16[3,8,256]{2,1,0:T(8,128)(2,1)S(1)} %get-tuple-element.334), channel_id=1, source_target_pairs={{8,0},{16,8},{24,16},{32,24},{40,32},{48,40},{56,48},{64,56},{72,6... | collective-permute-start | bytes 36872 | tf_op jit(solution)/shard_map/ppermute | solution.py:25
  185.3 8.1 %collective-permute-start.10 = (bf16[14,3,256]{2,1,0:T(4,128)(2,1)}, bf16[14,3,256]{2,1,0:T(4,128)(2,1)S(1)}, u32[]{:S(2)}, u32[]{:S(2)}) collective-permute-start(bf16[14,3,256]{2,1,0:T(4,128)(2,1)} %get-tuple-element.219), channel_id=1, source_target_pairs={{0,1},{1,2},{2,3},{3,4},{4,5},{5,6},{6,7},{7,0},{8,9},{9,10},{10,1... | collective-permute-start | bytes 64520 | tf_op jit(solution)/shard_map/ppermute | solution.py:24
  185.3 8.1 %collective-permute-start.11 = (bf16[14,3,256]{2,1,0:T(4,128)(2,1)}, bf16[14,3,256]{2,1,0:T(4,128)(2,1)}, u32[]{:S(2)}, u32[]{:S(2)}) collective-permute-start(bf16[14,3,256]{2,1,0:T(4,128)(2,1)} %get-tuple-element.220), channel_id=1, source_target_pairs={{1,0},{2,1},{3,2},{4,3},{5,4},{6,5},{7,6},{0,7},{9,8},{10,9},{11,1... | collective-permute-start | bytes 64520 | tf_op jit(solution)/shard_map/ppermute | solution.py:25
  201.5 12.7 %collective-permute-start.12 = (bf16[3,8,256]{2,1,0:T(8,128)(2,1)S(1)}, bf16[3,8,256]{2,1,0:T(8,128)(2,1)S(1)}, u32[]{:S(2)}, u32[]{:S(2)}) collective-permute-start(bf16[3,8,256]{2,1,0:T(8,128)(2,1)S(1)} %get-tuple-element.331), channel_id=1, source_target_pairs={{0,8},{8,16},{16,24},{24,32},{32,40},{40,48},{48,56},{56,64},{64,7... | collective-permute-start | bytes 36872 | tf_op jit(solution)/shard_map/ppermute | solution.py:24
  201.5 12.7 %collective-permute-start.13 = (bf16[3,8,256]{2,1,0:T(8,128)(2,1)S(1)}, bf16[3,8,256]{2,1,0:T(8,128)(2,1)S(1)}, u32[]{:S(2)}, u32[]{:S(2)}) collective-permute-start(bf16[3,8,256]{2,1,0:T(8,128)(2,1)S(1)} %get-tuple-element.332), channel_id=1, source_target_pairs={{8,0},{16,8},{24,16},{32,24},{40,32},{48,40},{56,48},{64,56},{72,6... | collective-permute-start | bytes 36872 | tf_op jit(solution)/shard_map/ppermute | solution.py:25
  214.2 4.3 collective-permute-start.14
  214.3 4.2 collective-permute-start.15
  (128 other events, 1159.6 us)
Sparse Core Ops, SparseCore 0:
  222.3 279.1 all-reduce.3
where the time goes:
time: 518 us; the launch traced here: 516 us
  waiting for transfers between devices  251 us (48%)
  blocking collectives  85.8 us (17%)
  starting transfers between devices  64.5 us (12%)
  local copies, waits for them, and re-layouts  47.1 us (9%)
  matrix products  26.6 us (5%)
  other arithmetic  23.1 us (4%)
  between operations  16.7 us (3%)
    psum x1, waiting for transfers between devices, on_device(): lax.psum((g_embed, g_patch, grad_kernel, grad_expand, grad_reduce), ('dp'...  190 us
    psum x1, blocking collectives, on_device(): lax.psum((g_embed, g_patch, grad_kernel, grad_expand, grad_reduce), ('dp'...  85.8 us
    all_to_all x1, waiting for transfers between devices, on_device(): lax.all_to_all(send_values.astype(jnp.float32), ('lon', 'lat'), split_axi...  45.4 us
    ppermute x8, starting transfers between devices, padded_2(): after = lax.ppermute(leading, axis, down)  28.8 us
    all_to_all x1, starting transfers between devices, on_device(): lax.all_to_all(send_counts, ('lon', 'lat'), split_axis=0, concat_axis=0,...  16.3 us
    dot_general x16, matrix products, encode_group(): lax.dot_general(lat_factor, flat, (((1,), (1,)), ((), ())), preferred_ele...  13.1 us
    all_to_all x1, starting transfers between devices, on_device(): lax.all_to_all(send_coords, ('lon', 'lat'), split_axis=0, concat_axis=0,...  11.2 us
    unnamed x348, local copies, waits for them, and re-layouts  10.5 us
  transfers between devices with their start and end apart: 20, of which 9 were waited for; matrix products, arithmetic and copies ran while one was open for 8% of the time, Pallas kernels for 0%

commit v1 on v0

v1 whole, which is shorter than its diff:
```python
import functools
import math

import jax
import jax.numpy as jnp
from jax import lax
from jax.experimental import pallas as pl
from jax.experimental.pallas import tpu as pltpu
from jax.sharding import PartitionSpec as P

MESH = pl.DeviceIdType.MESH
F32 = jnp.float32
BF16 = jnp.bfloat16
OBSF = 16
KSIDE = 7
REACH = 3
TILE = 16
SIDE = 8
CELLS = 64
CH = 256
HID = 1024
INVERSE = 0.5 / (0.7 * 0.7)
PADW = 16
NT = (((1,), (1,)), ((), ()))
TN = (((0,), (0,)), ((), ()))


def dot(a, b, dims=(((1,), (0,)), ((), ()))):
    return lax.dot_general(a, b, dims, preferred_element_type=F32)


def encode_kernel(nx, ny, nz, dest_ref, count_ref, values_ref, coords_ref, p0_ref, p1_ref, dens_ref):
    p0_ref[...] = jnp.zeros_like(p0_ref)
    p1_ref[...] = jnp.zeros_like(p1_ref)
    dens_ref[...] = jnp.zeros_like(dens_ref)
    rows = values_ref.shape[2]
    order = lax.broadcasted_iota(jnp.int32, (TILE, rows), 0)
    cell = (2 * (order % SIDE) + order // SIDE).astype(F32)
    lane = lax.broadcasted_iota(jnp.int32, (TILE, rows), 1)
    ones = jnp.ones((OBSF, rows), BF16)

    def one_block(block, carry):
        tile = dest_ref[block]
        pair = coords_ref[block]
        a = jnp.exp(-jnp.square(pair[0:1, :] - cell) * INVERSE)
        a = jnp.where(lane < count_ref[block], a, 0.0)
        b = jnp.exp(-jnp.square(pair[1:2, :] - cell) * INVERSE)
        parts = []
        for i in range(2):
            for j in range(2):
                left = a[i * SIDE : (i + 1) * SIDE]
                right = b[j * SIDE : (j + 1) * SIDE]
                parts.append((left[:, None, :] * right[None]).reshape(CELLS, rows))
        weight = jnp.concatenate(parts, axis=0).astype(BF16)
        sums = dot(jnp.concatenate([values_ref[block], ones], axis=0), weight, NT)
        lon = tile // nz
        lat = tile % nz
        x = lon // ny
        y = lon % ny
        p0_ref[lon * (nz + 1) + lat] = sums[:OBSF, :128].astype(BF16)
        p1_ref[(y * nx + x) * nz + lat] = sums[:OBSF, 128:].astype(BF16)
        dens_ref[lon, pl.ds(lat, 1), :] = sums[OBSF : OBSF + 1, :128]
        dens_ref[lon, pl.ds(SIDE + lat, 1), :] = sums[OBSF : OBSF + 1, 128:]
        return carry

    lax.fori_loop(0, values_ref.shape[0], one_block, 0, unroll=2)
    for lon in range(nx * ny):
        p0_ref[lon * (nz + 1) + nz] = dens_ref[lon].astype(BF16)


def encode(nx, ny, nz, dest, count, values, coords):
    lon = nx * ny
    return pl.pallas_call(
        functools.partial(encode_kernel, nx, ny, nz),
        out_shape=(
            jax.ShapeDtypeStruct((lon * (nz + 1), 16, 128), BF16),
            jax.ShapeDtypeStruct((lon * nz, 16, 128), BF16),
        ),
        in_specs=[pl.BlockSpec(memory_space=pltpu.SMEM)] * 2 + [pl.BlockSpec(memory_space=pltpu.VMEM)] * 2,
        out_specs=(pl.BlockSpec(memory_space=pltpu.VMEM),) * 2,
        scratch_shapes=[pltpu.VMEM((lon, 16, 128), F32)],
        compiler_params=pltpu.CompilerParams(vmem_limit_bytes=32 * 2**20),
    )(dest, count, values, coords)


def normalise(field):
    center = jnp.mean(field, axis=-1, keepdims=True)
    shifted = field - center
    scale = lax.rsqrt(jnp.mean(jnp.square(shifted), axis=-1, keepdims=True) + 1e-05)
    return shifted * scale, scale


def normalise_grad(normed, scale, grad):
    return scale * (
        grad
        - jnp.mean(grad, axis=-1, keepdims=True)
        - normed * jnp.mean(grad * normed, axis=-1, keepdims=True)
    )


def cdf(field):
    return 0.5 * (1.0 + lax.erf(field * math.sqrt(0.5)))


def group_sizes(nx, ny, nz, np_half, nq_half):
    return np_half // (nx * ny), nq_half // (nx * ny)


def group_scratch(nx, ny, nz, n_p, n_q, scatter):
    up, uq = n_p // (nx * ny), n_q // (nx * ny)

    def units(*lead):
        return pltpu.VMEM(tuple(lead) + (16, 128), BF16)

    plan = {
        "gp": units(2, n_p), "gq": units(2, n_q),
        "cp": units(n_p), "cq": units(n_q),
        "sp": units(n_p), "sq": units(n_q),
        "l1p": units(nx - 1, n_p // nx), "l1q": units(ny - 1, n_q // ny),
        "s2p": units(n_p // nx), "s2q": units(n_q // ny),
        "l2p": units(ny - 1, up), "l2q": units(nx - 1, uq),
        "s3": units(up + uq),
        "fp": units(2, n_p), "fq": units(2, n_q),
    }
    if scatter:
        piece = (up + uq) // nz
        plan["l3"] = units(nz - 1, piece)
        plan["f3"] = units(nz, piece)
    else:
        plan["l3"] = units(nz, up + uq)
    return plan


GROUPS = (("A", 64, 64, True), ("B", 64, 64, True), ("C", 64, 16, False))


def scratch_plan(nx, ny, nz):
    def units(*lead):
        return pltpu.VMEM(tuple(lead) + (16, 128), BF16)

    plan = {
        "r0": units(nx - 1, ny * (nz + 1)), "r1": units(ny - 1, nx * nz),
        "q0": units(ny * (nz + 1)), "q1": units(nx * nz),
        "t0": units(ny - 1, nz + 1), "t1": units(nx - 1, nz),
        "zbuf": units(nz, 3), "zr": units(nz - 1, 3),
        "dens": pltpu.VMEM((16, 128), F32),
        "ew": pltpu.VMEM((32, CH), F32),
        "kg": pltpu.VMEM((112, CH), F32),
        "eg": pltpu.VMEM((32, CH), F32),
        "tap": pltpu.VMEM((KSIDE * KSIDE, 8, CH), F32),
    }
    for k in range(4):
        plan["halo_src%d" % k] = pltpu.VMEM((2, CELLS, CH), BF16)
        plan["halo_dst%d" % k] = pltpu.VMEM((8, CELLS // 2, CH), BF16)
        plan["pad%d" % k] = pltpu.VMEM((2, 14 * PADW, 128), F32)
    plan["cols"] = pltpu.VMEM((CELLS, CH), F32)
    for name, n_p, n_q, scatter in GROUPS:
        for key, value in group_scratch(nx, ny, nz, n_p, n_q, scatter).items():
            plan[name + key] = value
    return plan


def copy_count(nx, ny, nz):
    total = 2 * (nx + ny - 2) + (nz - 1) + 4 * 8
    for _, _, _, scatter in GROUPS:
        total += 2 * 2 + 4 * (nx + ny - 2) + (nz - 1) * (2 if scatter else 1)
    return total


HALOS = tuple((i, j) for i in (-1, 0, 1) for j in (-1, 0, 1) if (i, j) != (0, 0))


def net_kernel(nx, ny, nz, names, *refs):
    (p0, p1, embed_w, patch_w, depth_k, expand_w, reduce_w, cot,
     feat, o_embed, o_patch, o_kernel, o_expand, o_reduce) = refs[:14]
    s = dict(zip(names, refs[14:]))
    send_sem, recv_sem = refs[14 + len(names):]
    core = lax.axis_index("dp")
    lon = lax.axis_index("lon")
    z = lax.axis_index("lat")
    x = lon // ny
    y = lon % ny
    nlon = nx * ny

    def at_core():
        return (1 - core, lon, z)

    def at_x(d):
        return (core, ((x + d) % nx) * ny + y, z)

    def at_y(d):
        return (core, x * ny + (y + d) % ny, z)

    def at_z(d):
        return (core, lon, (z + d) % nz)

    def at_halo(i, j):
        return (core, (lon + i + nlon) % nlon, (z + j + nz) % nz)

    barrier = pltpu.get_barrier_semaphore()
    peers = [at_core()] + [at_x(d) for d in range(1, nx)] + [at_y(d) for d in range(1, ny)]
    peers += [at_z(d) for d in range(1, nz)] + [at_halo(i, j) for i, j in HALOS]
    for peer in peers:
        pl.semaphore_signal(barrier, inc=1, device_id=peer, device_id_type=MESH)
    pl.semaphore_wait(barrier, len(peers))

    sent = []

    def push(src, dst, device, land=None):
        index = len(sent)

        def make(target):
            return pltpu.make_async_remote_copy(
                src_ref=src, dst_ref=target, send_sem=send_sem.at[index], recv_sem=recv_sem.at[index],
                device_id=device, device_id_type=MESH,
            )

        copy = make(dst)
        copy.start()
        sent.append(copy)
        return copy if land is None else make(land)

    def settle(copies):
        for copy in copies:
            copy.wait_recv()

    def spread(src, land, size, count, target):
        position = {"x": x, "y": y}[target]
        where = {"x": at_x, "y": at_y}[target]
        return [
            push(src.at[pl.ds(((position + d) % count) * size, size)], land.at[d - 1], where(d))
            for d in range(1, count)
        ]

    def fold(out, first, land, count, offset, size, step):
        for i in range(0, size, step):
            total = first[pl.ds(offset + i, step)].astype(F32)
            for d in range(count - 1):
                total = total + land[d, i : i + step].astype(F32)
            out[i : i + step] = total.astype(BF16)

    w0, w1 = nz + 1, nz
    copies = spread(p0, s["r0"], ny * w0, nx, "x") + spread(p1, s["r1"], nx * w1, ny, "y")
    s["ew"][...] = jnp.zeros_like(s["ew"])
    s["ew"][0 : OBSF + 1, :] = embed_w[...].astype(F32)
    s["kg"][...] = jnp.zeros_like(s["kg"])
    embed_m = s["ew"][...].astype(BF16)
    settle(copies)
    fold(s["q0"], p0, s["r0"], nx, x * (ny * w0), ny * w0, w0)
    fold(s["q1"], p1, s["r1"], ny, y * (nx * w1), nx * w1, w1)
    copies = spread(s["q0"], s["t0"], w0, ny, "y") + spread(s["q1"], s["t1"], w1, nx, "x")
    settle(copies)
    total0 = s["q0"][pl.ds(y * w0, w0)].astype(F32)
    for d in range(ny - 1):
        total0 = total0 + s["t0"][d].astype(F32)
    total0 = total0.astype(BF16)
    total1 = s["q1"][pl.ds(x * w1, w1)].astype(F32)
    for d in range(nx - 1):
        total1 = total1 + s["t1"][d].astype(F32)
    total1 = total1.astype(BF16)
    for k in range(nz):
        s["zbuf"][k, 0] = total0[k]
        s["zbuf"][k, 1] = total1[k]
        s["zbuf"][k, 2] = total0[nz]
    copies = [push(s["zbuf"].at[(z + d) % nz], s["zr"].at[d - 1], at_z(d)) for d in range(1, nz)]
    settle(copies)
    sums = s["zbuf"][z].astype(F32)
    for d in range(nz - 1):
        sums = sums + s["zr"][d].astype(F32)
    s["dens"][...] = sums[2]
    density = jnp.concatenate([s["dens"][pl.ds(z, 1), :], s["dens"][pl.ds(SIDE + z, 1), :]], axis=1)
    scaled = jnp.concatenate([sums[0], sums[1]], axis=1) * lax.rsqrt(1.0 + density)
    level = jnp.where(
        lax.broadcasted_iota(jnp.int32, (16, CH), 0) == 0,
        jnp.broadcast_to(0.25 * jnp.log(1.0 + density), (16, CH)), 0.0,
    )
    encoded = jnp.concatenate([scaled, level], axis=0).astype(BF16)

    grid_hat, grid_scale = normalise(dot(encoded, embed_m, TN))
    normed_grid = grid_hat.astype(BF16)
    first = jnp.zeros((CELLS, CH), F32)
    for i in range(4):
        first = first + dot(normed_grid[i * CELLS : (i + 1) * CELLS], patch_w[i * CH : (i + 1) * CH, :])
    state = first.astype(BF16)

    def halo_send(which, field):
        src, dst = s["halo_src%d" % which], s["halo_dst%d" % which]
        src[0] = field.astype(BF16)
        src[1] = jnp.swapaxes(field.reshape(SIDE, SIDE, CH), 0, 1).reshape(CELLS, CH).astype(BF16)
        found = []
        for index, (i, j) in enumerate(HALOS):
            if j == 0:
                piece = src.at[0, pl.ds(32 if i > 0 else 0, 32)]
            else:
                piece = src.at[1, pl.ds(32 if j > 0 else 0, 32)]
            found.append(push(piece, dst.at[index], at_halo(i, j)))
        return found

    def pad_inner(which, field):
        pad = s["pad%d" % which]
        pad[...] = jnp.zeros_like(pad)
        for p in range(SIDE):
            for h in range(2):
                pad[h, pl.ds((REACH + p) * PADW + REACH, SIDE), :] = field[
                    p * SIDE : (p + 1) * SIDE, h * 128 : (h + 1) * 128
                ]

    def halo_wait(which, copies):
        pad, dst = s["pad%d" % which], s["halo_dst%d" % which]
        settle(copies)
        for index, (i, j) in enumerate(HALOS):
            if j == 0:
                for r in range(REACH):
                    if i > 0:
                        row, at = r, 1 + r
                    else:
                        row, at = REACH + SIDE + r, r
                    strip = dst[index].astype(F32)[at * SIDE : (at + 1) * SIDE]
                    for h in range(2):
                        pad[h, pl.ds(row * PADW + REACH, SIDE), :] = strip[:, h * 128 : (h + 1) * 128]
                continue
            inside = (z > 0) if j > 0 else (z < nz - 1)
            keep = jnp.where(inside, 1.0, 0.0).astype(F32)
            block = dst[index].astype(F32) * keep
            for r in range(REACH):
                if j > 0:
                    column, at = r, 1 + r
                else:
                    column, at = REACH + SIDE + r, r
                strip = block[at * SIDE : (at + 1) * SIDE]
                if i == 0:
                    top, strip = REACH, strip
                elif i > 0:
                    top, strip = 0, strip[SIDE - REACH :]
                else:
                    top, strip = REACH + SIDE, strip[:REACH]
                for h in range(2):
                    pad[h, pl.ds(top * PADW + column, strip.shape[0], PADW), :] = strip[:, h * 128 : (h + 1) * 128]

    def window(which, column):
        pad = s["pad%d" % which]
        return jnp.stack(
            [
                jnp.concatenate([pad[h, pl.ds(p * PADW + column, SIDE), :] for h in range(2)], axis=1)
                for p in range(14)
            ],
            axis=0,
        )

    def convolve(which, kernel, flip):
        total = jnp.zeros((SIDE, SIDE, CH), F32)
        for b in range(KSIDE):
            part = window(which, b)
            for a in range(KSIDE):
                tap = KSIDE * a + b
                if flip:
                    tap = KSIDE * KSIDE - 1 - tap
                total = total + part[a : a + SIDE] * kernel[tap : tap + 1, :].reshape(1, 1, CH)
        return total.reshape(CELLS, CH)

    def kernel_grad(which, grad, row):
        grad = grad.reshape(SIDE, SIDE, CH)
        for b in range(KSIDE):
            part = window(which, b)
            for a in range(KSIDE):
                s["tap"][KSIDE * a + b] = jnp.sum(part[a : a + SIDE] * grad, axis=0)
        s["kg"][row : row + KSIDE * KSIDE, :] = jnp.sum(s["tap"][...], axis=1)

    stored = []
    for k in range(2):
        field = state.astype(F32)
        copies = halo_send(k, field)
        pad_inner(k, field)
        kernel = depth_k[k].astype(F32)
        halo_wait(k, copies)
        hat, scale = normalise(convolve(k, kernel, False))
        normed = hat.astype(BF16)
        act = dot(normed, expand_w[k])
        share = cdf(act)
        hidden = (act * share).astype(BF16)
        state = (field + dot(hidden, reduce_w[k])).astype(BF16)
        slope = share + act * jnp.exp(-0.5 * jnp.square(act)) * (1.0 / math.sqrt(2.0 * math.pi))
        stored.append((hat, scale, normed, hidden, slope))
    feat[...] = state

    progress = {}

    def group(name):
        return next(entry for entry in GROUPS if entry[0] == name)

    def begin(name):
        gp, gq = s[name + "gp"], s[name + "gq"]
        progress[name] = [
            push(gp.at[1 - core], s[name + "cp"], at_core()),
            push(gq.at[1 - core], s[name + "cq"], at_core()),
        ]

    def stage_first(name):
        _, n_p, n_q, _ = group(name)
        settle(progress[name])
        for key, n in (("p", n_p), ("q", n_q)):
            own, got, out = s[name + "g" + key], s[name + "c" + key], s[name + "s" + key]

            def body(i, carry, own=own, got=got, out=out):
                at = pl.ds(pl.multiple_of(i * 8, 8), 8)
                out[at] = (own[core, at].astype(F32) + got[at].astype(F32)).astype(BF16)
                return carry

            lax.fori_loop(0, n // 8, body, 0)
        progress[name] = spread(s[name + "sp"], s[name + "l1p"], n_p // nx, nx, "x") + spread(
            s[name + "sq"], s[name + "l1q"], n_q // ny, ny, "y"
        )

    def stage_second(name):
        _, n_p, n_q, _ = group(name)
        settle(progress[name])
        fold(s[name + "s2p"], s[name + "sp"], s[name + "l1p"], nx, x * (n_p // nx), n_p // nx, min(8, n_p // nx))
        fold(s[name + "s2q"], s[name + "sq"], s[name + "l1q"], ny, y * (n_q // ny), n_q // ny, min(8, n_q // ny))
        progress[name] = spread(s[name + "s2p"], s[name + "l2p"], n_p // nlon, ny, "y") + spread(
            s[name + "s2q"], s[name + "l2q"], n_q // nlon, nx, "x"
        )

    def stage_third(name):
        _, n_p, n_q, scatter = group(name)
        up, uq = n_p // nlon, n_q // nlon
        settle(progress[name])
        s3 = s[name + "s3"]
        fold(s3.at[pl.ds(0, up)], s[name + "s2p"], s[name + "l2p"], ny, y * up, up, min(8, up))
        fold(s3.at[pl.ds(up, uq)], s[name + "s2q"], s[name + "l2q"], nx, x * uq, uq, min(8, uq))
        l3 = s[name + "l3"]
        if scatter:
            piece = (up + uq) // nz
            progress[name] = [
                push(s3.at[pl.ds(((z + d) % nz) * piece, piece)], l3.at[d - 1], at_z(d)) for d in range(1, nz)
            ]
        else:
            l3[z] = s3[...]
            progress[name] = [push(s3, l3.at[z], at_z(d), l3.at[(z + nz - d) % nz]) for d in range(1, nz)]

    def stage_gather(name):
        _, n_p, n_q, _ = group(name)
        piece = (n_p + n_q) // (nlon * nz)
        settle(progress[name])
        s3, l3, f3 = s[name + "s3"], s[name + "l3"], s[name + "f3"]
        total = s3[pl.ds(z * piece, piece)].astype(F32)
        for d in range(nz - 1):
            total = total + l3[d].astype(F32)
        f3[z] = total.astype(BF16)
        progress[name] = [push(f3.at[z], f3.at[z], at_z(d), f3.at[(z + nz - d) % nz]) for d in range(1, nz)]

    def stage_back_second(name):
        _, n_p, n_q, scatter = group(name)
        up, uq = n_p // nlon, n_q // nlon
        settle(progress[name])
        fp, fq = s[name + "fp"], s[name + "fq"]
        at_p, at_q = x * (n_p // nx) + y * up, y * (n_q // ny) + x * uq
        if scatter:
            done = s[name + "f3"][...].reshape(up + uq, 16, 128)
        else:
            total = s[name + "l3"][0].astype(F32)
            for d in range(1, nz):
                total = total + s[name + "l3"][d].astype(F32)
            done = total.astype(BF16)
        fp[core, pl.ds(at_p, up)] = done[:up]
        fq[core, pl.ds(at_q, uq)] = done[up:]

        def from_p(d):
            return fp.at[core, pl.ds(x * (n_p // nx) + ((y + ny - d) % ny) * up, up)]

        def from_q(d):
            return fq.at[core, pl.ds(y * (n_q // ny) + ((x + nx - d) % nx) * uq, uq)]

        progress[name] = [push(from_p(0), from_p(0), at_y(d), from_p(d)) for d in range(1, ny)]
        progress[name] += [push(from_q(0), from_q(0), at_x(d), from_q(d)) for d in range(1, nx)]

    def stage_back_first(name):
        _, n_p, n_q, _ = group(name)
        settle(progress[name])
        fp, fq = s[name + "fp"], s[name + "fq"]
        hp, hq = n_p // nx, n_q // ny

        def from_p(d):
            return fp.at[core, pl.ds(((x + nx - d) % nx) * hp, hp)]

        def from_q(d):
            return fq.at[core, pl.ds(((y + ny - d) % ny) * hq, hq)]

        progress[name] = [push(from_p(0), from_p(0), at_x(d), from_p(d)) for d in range(1, nx)]
        progress[name] += [push(from_q(0), from_q(0), at_y(d), from_q(d)) for d in range(1, ny)]

    def stage_back_core(name):
        settle(progress[name])
        fp, fq = s[name + "fp"], s[name + "fq"]
        progress[name] = [
            push(fp.at[core], fp.at[core], at_core(), fp.at[1 - core]),
            push(fq.at[core], fq.at[core], at_core(), fq.at[1 - core]),
        ]

    def write_tall(out, fp):
        for h in range(2):
            for r in range(0, 64, 8):
                out[r * 16 : (r + 8) * 16, h * 128 : (h + 1) * 128] = fp[h, r : r + 8].astype(F32).reshape(128, 128)

    def finish(name):
        settle(progress[name])
        fp, fq = s[name + "fp"], s[name + "fq"]
        if name == "C":
            write_tall(o_patch, fp)
            for h in range(2):
                at = slice(h * 128, (h + 1) * 128)
                s["kg"][:, at] = fq[h, 0:7].astype(F32).reshape(112, 128)
                s["eg"][:, at] = fq[h, 7:9].astype(F32).reshape(32, 128)
            o_kernel[0] = s["kg"][0:49, :]
            o_kernel[1] = s["kg"][49:98, :]
            o_embed[...] = s["eg"][0 : OBSF + 1, :]
            return
        k = 1 if name == "A" else 0
        write_tall(o_reduce.at[k], fp)
        for lane in range(8):
            part = fq[lane // 4, (lane % 4) * 16 : (lane % 4 + 1) * 16]
            o_expand[k, :, lane * 128 : (lane + 1) * 128] = part.astype(F32).reshape(256, 128)

    def put_tall(name, left, right):
        for h in range(2):
            s[name + "gp"][h] = dot(left, right[:, h * 128 : (h + 1) * 128], TN).astype(BF16).reshape(64, 16, 128)

    def put_wide(name, left, right):
        for lane in range(8):
            part = dot(left, right[:, lane * 128 : (lane + 1) * 128], TN).astype(BF16)
            s[name + "gq"][lane // 4, (lane % 4) * 16 : (lane % 4 + 1) * 16] = part.reshape(16, 16, 128)

    cotangent = cot[...]
    for k in (1, 0):
        name = "A" if k == 1 else "B"
        hat, scale, normed, hidden, slope = stored[k]
        grad_act = (dot(cotangent, reduce_w[k], NT) * slope).astype(BF16)
        grad_depth = normalise_grad(hat, scale, dot(grad_act, expand_w[k], NT))
        copies = halo_send(2 + k, grad_depth)
        put_tall(name, hidden, cotangent)
        put_wide(name, normed, grad_act)
        begin(name)
        if k == 0:
            stage_second("A")
        pad_inner(2 + k, grad_depth)
        kernel_grad(k, grad_depth, k * KSIDE * KSIDE)
        halo_wait(2 + k, copies)
        cotangent = (cotangent.astype(F32) + convolve(2 + k, depth_k[k].astype(F32), True)).astype(BF16)
        if k == 0:
            stage_third("A")
        stage_first(name)

    parts = []
    for i in range(4):
        piece = normed_grid[i * CELLS : (i + 1) * CELLS]
        grad = dot(piece, cotangent, TN).astype(BF16)
        for h in range(2):
            s["Cgp"][h, i * 16 : (i + 1) * 16] = grad[:, h * 128 : (h + 1) * 128].reshape(16, 16, 128)
        parts.append(dot(cotangent, patch_w[i * CH : (i + 1) * CH, :], NT))
    grad_grid = normalise_grad(grid_hat, grid_scale, jnp.concatenate(parts, axis=0)).astype(BF16)
    grad_embed = dot(encoded, grad_grid).astype(BF16)
    grad_taps = s["kg"][...].astype(BF16)
    for h in range(2):
        at = slice(h * 128, (h + 1) * 128)
        s["Cgq"][h, 0:7] = grad_taps[:, at].reshape(7, 16, 128)
        s["Cgq"][h, 7:9] = grad_embed[:, at].reshape(2, 16, 128)
        s["Cgq"][h, 9:16] = jnp.zeros((7, 16, 128), BF16)
    begin("C")
    stage_gather("A")
    stage_second("B")
    stage_first("C")
    stage_back_second("A")
    stage_third("B")
    stage_second("C")
    stage_back_first("A")
    stage_gather("B")
    stage_third("C")
    stage_back_core("A")
    stage_back_second("B")
    stage_back_second("C")
    finish("A")
    stage_back_first("B")
    stage_back_first("C")
    stage_back_core("B")
    stage_back_core("C")
    finish("B")
    finish("C")
    for copy in sent:
        copy.wait_send()


def factor(lon):
    nx = math.isqrt(lon)
    while lon % nx:
        nx -= 1
    return nx, lon // nx


def on_device(values, coords, dest, count, embed_w, patch_w, depth_k, expand_w, reduce_w, cot):
    nx, ny = factor(lax.axis_size("lon"))
    nz = lax.axis_size("lat")
    p0, p1 = encode(nx, ny, nz, dest[0, 0, 0], count[0, 0, 0], values[0, 0, 0], coords[0, 0, 0])
    plan = scratch_plan(nx, ny, nz)
    copies = copy_count(nx, ny, nz)
    vmem = pl.BlockSpec(memory_space=pltpu.VMEM)
    outs = pl.pallas_call(
        functools.partial(net_kernel, nx, ny, nz, tuple(plan)),
        out_shape=(
            jax.ShapeDtypeStruct((CELLS, CH), BF16),
            jax.ShapeDtypeStruct((OBSF + 1, CH), F32),
            jax.ShapeDtypeStruct((4 * CH, CH), F32),
            jax.ShapeDtypeStruct((2, KSIDE * KSIDE, CH), F32),
            jax.ShapeDtypeStruct((2, CH, HID), F32),
            jax.ShapeDtypeStruct((2, HID, CH), F32),
        ),
        in_specs=[vmem] * 8,
        out_specs=(vmem,) * 6,
        scratch_shapes=list(plan.values())
        + [pltpu.SemaphoreType.DMA((copies,)), pltpu.SemaphoreType.DMA((copies,))],
        compiler_params=pltpu.CompilerParams(
            collective_id=0, has_side_effects=True, vmem_limit_bytes=56 * 2**20
        ),
    )(p0, p1, embed_w, patch_w, depth_k, expand_w, reduce_w, cot[0].reshape(CELLS, CH))
    return (outs[0].reshape(1, SIDE, SIDE, CH),) + tuple(outs[1:])


def solution(mesh):
    in_specs = (
        P("dp", "lon", "lat", None, None, None),
        P("dp", "lon", "lat", None, None, None),
        P("dp", "lon", "lat", None),
        P("dp", "lon", "lat", None),
        P(),
        P(),
        P(),
        P(),
        P(),
        P("dp", "lon", "lat", None),
    )
    out_specs = (P("dp", "lon", "lat", None), P(), P(), P(), P(), P())
    return jax.shard_map(
        on_device, mesh=mesh, in_specs=in_specs, out_specs=out_specs, check_vma=False
    )
```

time: 518 us -> 126 us (0.24)
  waiting for transfers between devices: 251 us -> 0 us
  Pallas kernels: 0 us -> 108 us
  blocking collectives: 85.8 us -> 0 us
  starting transfers between devices: 64.5 us -> 0 us
  local copies, waits for them, and re-layouts: 47.1 us -> 16.9 us
  matrix products: 26.6 us -> 0 us
  other arithmetic: 23.1 us -> 0 us
  between operations: 16.7 us -> 0.67 us
    psum x1 -> x0, waiting for transfers between devices: 190 us -> none  [on_device(): lax.psum((g_embed, g_patch, grad_kernel, grad_expand, grad_reduce), ('dp'...]
    pallas_call x0 -> x2, Pallas kernels: none -> 108 us  [the longest x1 97.4 us: on_device(): pl.pallas_call(functools.partial(net_kernel, nx, ny, nz, tuple(plan)), ou...]
    psum x1 -> x0, blocking collectives: 85.8 us -> none  [on_device(): lax.psum((g_embed, g_patch, grad_kernel, grad_expand, grad_reduce), ('dp'...]
    all_to_all x3 -> x0, waiting for transfers between devices: 56.4 us -> none  [the longest x1 45.4 us: on_device(): lax.all_to_all(send_values.astype(jnp.float32), ('lon', 'lat'), split_axi...]
    all_to_all x3 -> x0, starting transfers between devices: 34 us -> none  [the longest x1 16.3 us: on_device(): lax.all_to_all(send_counts, ('lon', 'lat'), split_axis=0, concat_axis=0,...]
    ppermute x16 -> x0, starting transfers between devices: 30.5 us -> none  [the longest x8 28.8 us: padded_2(): after = lax.ppermute(leading, axis, down)]
    dot_general x33 -> x0, matrix products: 26.6 us -> none  [the longest x16 13.1 us: encode_group(): lax.dot_general(lat_factor, flat, (((1,), (1,)), ((), ())), preferred_ele...]
    scatter x3 -> x0, local copies, waits for them, and re-layouts: 16.5 us -> none  [the longest x1 8.14 us: on_device(): send_values = jnp.zeros((tile_count,) + block_values.shape[1:], block_val...]
  transfers between devices with their start and end apart: 20 -> 0, of which waited for: 9 -> 0; matrix products, arithmetic and copies ran while one was open for 8% -> 0% of each run, Pallas kernels for 0% -> 0%
where the time goes in v1:
time: 126 us; the launch traced here: 125 us
  Pallas kernels  108 us (86%)
  local copies, waits for them, and re-layouts  16.9 us (13%)
    pallas_call x1, Pallas kernels, on_device(): pl.pallas_call(functools.partial(net_kernel, nx, ny, nz, tuple(plan)), ou...  97.4 us
    unnamed x23, local copies, waits for them, and re-layouts  16.9 us
    pallas_call x1, Pallas kernels, encode(): pl.pallas_call(functools.partial(encode_kernel, nx, ny, nz), out_shape=(j...  10.1 us

profile of v1, /device:TPU:1, one launch (start us, length us, event | category | flops | bytes accessed | tf_op | source)
XLA Modules:
  0.0 125.1 jit_solution(14887549393659755505)
XLA Ops:
  0.6 1.4 %copy.16.refs_4_ = bf16[2,49,256]{2,1,0:T(8,128)(2,1)} copy(bf16[2,49,256]{2,0,1:T(2,128)(2,1)} %param.16) | data formatting | bytes 100352 | tf_op args[6]
  2.1 0.0 copy-start
  2.1 1.2 copy-done
  3.3 0.0 copy-start.3
  3.3 0.9 copy-done.3
  4.2 0.0 copy-start.4
  4.2 0.7 copy-done.4
  4.9 0.0 copy-start.5
  4.9 0.7 copy-done.5
  5.6 10.1 %shard_map.145 = (bf16[144,16,128]{2,1,0:T(8,128)(2,1)S(1)}, bf16[128,16,128]{2,1,0:T(8,128)(2,1)S(1)}) custom-call(s32[64]{0:T(128)S(1)} %bitcast.8, s32[64]{0:T(128)S(1)} %bitcast.9, bf16[64,16,512]{2,1,0:T(8,128)(2,1)S(1)} %bitcast.6, f32[64,2,512]{2,1,0:T(2,128)S(1)} %bitcast.7), custom_call_target="tpu_custom_call" | custom-call | tf_op jit(solution)/shard_map/pallas_call | solution.py:73
  15.6 0.0 copy-start.1
  15.7 0.8 copy-done.1
  16.5 0.0 copy-start.2
  16.5 0.8 copy-done.2
  17.3 97.4 %shard_map.146 = (bf16[64,256]{1,0:T(8,128)(2,1)}, f32[17,256]{1,0:T(8,128)}, f32[1024,256]{1,0:T(8,128)}, f32[2,49,256]{2,1,0:T(8,128)}, f32[2,256,1024]{2,1,0:T(8,128)}, /*index=5*/f32[2,1024,256]{2,1,0:T(8,128)}) custom-call(bf16[144,16,128]{2,1,0:T(8,128)(2,1)} %copy-done.1, bf16[128,16,128]{2,1,0:T(8,128)(2,1)} %copy-done.2, bf16[17,256]{1,0:T(8,128)(2,1)} %refs_2_.1, ...), custom_call_target="tpu_custom_call" | custom-call | tf_op jit(solution)/shard_map/pallas_call | solution.py:605
  114.7 0.0 copy-start.7
  114.7 1.7 %copy.17 = f32[2,49,256]{2,0,1:T(2,128)} copy(f32[2,49,256]{2,1,0:T(8,128)} %get-tuple-element.25) | data formatting | bytes 200704
  116.5 1.4 %copy.23 = bf16[1,8,8,256]{3,2,1,0:T(8,128)(2,1)} copy(bf16[1,8,8,256]{3,2,1,0:T(8,128)(2,1)} %bitcast.11) | data formatting | bytes 65536
  117.8 1.3 %copy.24 = f32[17,256]{1,0:T(8,128)} copy(f32[17,256]{1,0:T(8,128)} %get-tuple-element.35) | data formatting | bytes 34816
  119.2 2.3 %copy.25 = f32[1024,256]{1,0:T(8,128)} copy(f32[1024,256]{1,0:T(8,128)} %get-tuple-element.36) | data formatting | bytes 2097152
  121.4 0.0 copy-done.7
  121.4 0.0 copy-start.6
  121.4 1.3 %copy.26 = f32[2,256,1024]{2,1,0:T(8,128)} copy(f32[2,256,1024]{2,1,0:T(8,128)S(1)} %copy-done.7) | data formatting | bytes 4194304
  122.8 1.0 copy-done.6
  123.8 1.3 %copy.27 = f32[2,1024,256]{2,1,0:T(8,128)} copy(f32[2,1024,256]{2,1,0:T(8,128)S(1)} %copy-done.6) | data formatting | bytes 4194304
Async XLA Ops:
  2.1 1.2 copy-start
  3.3 0.9 copy-start.3
  4.2 0.7 copy-start.4
  4.9 0.7 copy-start.5
  15.6 0.8 copy-start.1
  16.5 0.8 copy-start.2
  114.7 6.7 %copy-start.7 = (f32[2,256,1024]{2,1,0:T(8,128)S(1)}, f32[2,256,1024]{2,1,0:T(8,128)}, u32[]{:S(2)}) copy-start(f32[2,256,1024]{2,1,0:T(8,128)} %get-tuple-element.38) | copy-start | bytes 6291460
  121.4 2.3 %copy-start.6 = (f32[2,1024,256]{2,1,0:T(8,128)S(1)}, f32[2,1024,256]{2,1,0:T(8,128)}, u32[]{:S(2)}) copy-start(f32[2,1024,256]{2,1,0:T(8,128)} %get-tuple-element.39) | copy-start | bytes 6291460

commit v2 on v1

--- a/solution.py
+++ b/solution.py
@@ -29,7 +29,38 @@
     return lax.dot_general(a, b, dims, preferred_element_type=F32)
 
 
-def encode_kernel(nx, ny, nz, dest_ref, count_ref, values_ref, coords_ref, p0_ref, p1_ref, dens_ref):
+PARTS = 4
+
+
+def in_hbm(array):
+    return pltpu.with_memory_space_constraint(array, pltpu.HBM)
+
+
+def encode_kernel(
+    nx, ny, nz, dest_hbm, count_hbm, values_hbm, coords_hbm, p0_ref, p1_ref, dens_ref,
+    dest_ref, count_ref, values_ref, coords_ref, sems,
+):
+    blocks = values_ref.shape[0]
+    parts = PARTS if blocks % PARTS == 0 else 1
+    share = blocks // parts
+    small = [
+        pltpu.make_async_copy(dest_hbm, dest_ref, sems.at[0]),
+        pltpu.make_async_copy(count_hbm, count_ref, sems.at[1]),
+    ]
+    large = []
+    for part in range(parts):
+        at = pl.ds(part * share, share)
+        large.append(
+            (
+                pltpu.make_async_copy(values_hbm.at[at], values_ref.at[at], sems.at[2 + 2 * part]),
+                pltpu.make_async_copy(coords_hbm.at[at], coords_ref.at[at], sems.at[3 + 2 * part]),
+            )
+        )
+    for copy in small:
+        copy.start()
+    for pair in large:
+        for copy in pair:
+            copy.start()
     p0_ref[...] = jnp.zeros_like(p0_ref)
     p1_ref[...] = jnp.zeros_like(p1_ref)
     dens_ref[...] = jnp.zeros_like(dens_ref)
@@ -63,7 +94,12 @@
         dens_ref[lon, pl.ds(SIDE + lat, 1), :] = sums[OBSF : OBSF + 1, 128:]
         return carry
 
-    lax.fori_loop(0, values_ref.shape[0], one_block, 0, unroll=2)
+    for copy in small:
+        copy.wait()
+    for part in range(parts):
+        for copy in large[part]:
+            copy.wait()
+        lax.fori_loop(part * share, (part + 1) * share, one_block, 0, unroll=min(share, 4))
     for lon in range(nx * ny):
         p0_ref[lon * (nz + 1) + nz] = dens_ref[lon].astype(BF16)
 
@@ -76,11 +112,18 @@
             jax.ShapeDtypeStruct((lon * (nz + 1), 16, 128), BF16),
             jax.ShapeDtypeStruct((lon * nz, 16, 128), BF16),
         ),
-        in_specs=[pl.BlockSpec(memory_space=pltpu.SMEM)] * 2 + [pl.BlockSpec(memory_space=pltpu.VMEM)] * 2,
+        in_specs=[pl.BlockSpec(memory_space=pltpu.HBM)] * 4,
         out_specs=(pl.BlockSpec(memory_space=pltpu.VMEM),) * 2,
-        scratch_shapes=[pltpu.VMEM((lon, 16, 128), F32)],
-        compiler_params=pltpu.CompilerParams(vmem_limit_bytes=32 * 2**20),
-    )(dest, count, values, coords)
+        scratch_shapes=[
+            pltpu.VMEM((lon, 16, 128), F32),
+            pltpu.SMEM(dest.shape, jnp.int32),
+            pltpu.SMEM(count.shape, jnp.int32),
+            pltpu.VMEM(values.shape, values.dtype),
+            pltpu.VMEM(coords.shape, coords.dtype),
+            pltpu.SemaphoreType.DMA((2 + 2 * PARTS,)),
+        ],
+        compiler_params=pltpu.CompilerParams(vmem_limit_bytes=24 * 2**20),
+    )(*(in_hbm(leaf) for leaf in (dest, count, values, coords)))
 
 
 def normalise(field):
@@ -120,7 +163,6 @@
         "s2p": units(n_p // nx), "s2q": units(n_q // ny),
         "l2p": units(ny - 1, up), "l2q": units(nx - 1, uq),
         "s3": units(up + uq),
-        "fp": units(2, n_p), "fq": units(2, n_q),
     }
     if scatter:
         piece = (up + uq) // nz
@@ -131,7 +173,7 @@
     return plan
 
 
-GROUPS = (("A", 64, 64, True), ("B", 64, 64, True), ("C", 64, 16, False))
+GROUPS = (("A", 64, 64, True), ("B", 64, 64, True), ("C", 32, 48, False))
 
 
 def scratch_plan(nx, ny, nz):
@@ -145,8 +187,7 @@
         "zbuf": units(nz, 3), "zr": units(nz - 1, 3),
         "dens": pltpu.VMEM((16, 128), F32),
         "ew": pltpu.VMEM((32, CH), F32),
-        "kg": pltpu.VMEM((112, CH), F32),
-        "eg": pltpu.VMEM((32, CH), F32),
+        "kg": pltpu.VMEM((2, 112, 128), F32),
         "tap": pltpu.VMEM((KSIDE * KSIDE, 8, CH), F32),
     }
     for k in range(4):
@@ -167,14 +208,21 @@
     return total
 
 
+FINALS = ("Afp", "Afq", "Bfp", "Bfq", "Cfp", "Cfq")
 HALOS = tuple((i, j) for i in (-1, 0, 1) for j in (-1, 0, 1) if (i, j) != (0, 0))
 
 
 def net_kernel(nx, ny, nz, names, *refs):
-    (p0, p1, embed_w, patch_w, depth_k, expand_w, reduce_w, cot,
-     feat, o_embed, o_patch, o_kernel, o_expand, o_reduce) = refs[:14]
-    s = dict(zip(names, refs[14:]))
-    send_sem, recv_sem = refs[14 + len(names):]
+    p0, p1 = refs[:2]
+    feat = refs[8]
+    s = dict(zip(FINALS, refs[9:15]))
+    s.update(zip(names, refs[15:]))
+    local = refs[15 + len(names) : 21 + len(names)]
+    embed_w, patch_w, depth_k, expand_w, reduce_w, cot = local
+    send_sem, recv_sem, load_sem = refs[21 + len(names) :]
+    loads = [
+        pltpu.make_async_copy(far, near, load_sem.at[i]) for i, (far, near) in enumerate(zip(refs[2:8], local))
+    ]
     core = lax.axis_index("dp")
     lon = lax.axis_index("lon")
     z = lax.axis_index("lat")
@@ -241,7 +289,11 @@
 
     w0, w1 = nz + 1, nz
     copies = spread(p0, s["r0"], ny * w0, nx, "x") + spread(p1, s["r1"], nx * w1, ny, "y")
+    for load in loads:
+        load.start()
     s["ew"][...] = jnp.zeros_like(s["ew"])
+    for load in loads:
+        load.wait()
     s["ew"][0 : OBSF + 1, :] = embed_w[...].astype(F32)
     s["kg"][...] = jnp.zeros_like(s["kg"])
     embed_m = s["ew"][...].astype(BF16)
@@ -347,6 +399,9 @@
             axis=0,
         )
 
+    def taps_of(k):
+        return [depth_k[tap].astype(F32)[k : k + 1].reshape(1, 1, CH) for tap in range(KSIDE * KSIDE)]
+
     def convolve(which, kernel, flip):
         total = jnp.zeros((SIDE, SIDE, CH), F32)
         for b in range(KSIDE):
@@ -355,23 +410,25 @@
                 tap = KSIDE * a + b
                 if flip:
                     tap = KSIDE * KSIDE - 1 - tap
-                total = total + part[a : a + SIDE] * kernel[tap : tap + 1, :].reshape(1, 1, CH)
+                total = total + part[a : a + SIDE] * kernel[tap]
         return total.reshape(CELLS, CH)
 
-    def kernel_grad(which, grad, row):
+    def kernel_grad(which, grad):
         grad = grad.reshape(SIDE, SIDE, CH)
         for b in range(KSIDE):
             part = window(which, b)
             for a in range(KSIDE):
                 s["tap"][KSIDE * a + b] = jnp.sum(part[a : a + SIDE] * grad, axis=0)
-        s["kg"][row : row + KSIDE * KSIDE, :] = jnp.sum(s["tap"][...], axis=1)
+        taps = jnp.sum(s["tap"][...], axis=1)
+        for h in range(2):
+            s["kg"][h, pl.ds(which, KSIDE * KSIDE, 2), :] = taps[:, h * 128 : (h + 1) * 128]
 
     stored = []
     for k in range(2):
         field = state.astype(F32)
         copies = halo_send(k, field)
         pad_inner(k, field)
-        kernel = depth_k[k].astype(F32)
+        kernel = taps_of(k)
         halo_wait(k, copies)
         hat, scale = normalise(convolve(k, kernel, False))
         normed = hat.astype(BF16)
@@ -414,8 +471,8 @@
     def stage_second(name):
         _, n_p, n_q, _ = group(name)
         settle(progress[name])
-        fold(s[name + "s2p"], s[name + "sp"], s[name + "l1p"], nx, x * (n_p // nx), n_p // nx, min(8, n_p // nx))
-        fold(s[name + "s2q"], s[name + "sq"], s[name + "l1q"], ny, y * (n_q // ny), n_q // ny, min(8, n_q // ny))
+        fold(s[name + "s2p"], s[name + "sp"], s[name + "l1p"], nx, x * (n_p // nx), n_p // nx, math.gcd(8, n_p // nx))
+        fold(s[name + "s2q"], s[name + "sq"], s[name + "l1q"], ny, y * (n_q // ny), n_q // ny, math.gcd(8, n_q // ny))
         progress[name] = spread(s[name + "s2p"], s[name + "l2p"], n_p // nlon, ny, "y") + spread(
             s[name + "s2q"], s[name + "l2q"], n_q // nlon, nx, "x"
         )
@@ -425,8 +482,8 @@
         up, uq = n_p // nlon, n_q // nlon
         settle(progress[name])
         s3 = s[name + "s3"]
-        fold(s3.at[pl.ds(0, up)], s[name + "s2p"], s[name + "l2p"], ny, y * up, up, min(8, up))
-        fold(s3.at[pl.ds(up, uq)], s[name + "s2q"], s[name + "l2q"], nx, x * uq, uq, min(8, uq))
+        fold(s3.at[pl.ds(0, up)], s[name + "s2p"], s[name + "l2p"], ny, y * up, up, math.gcd(8, up))
+        fold(s3.at[pl.ds(up, uq)], s[name + "s2q"], s[name + "l2q"], nx, x * uq, uq, math.gcd(8, uq))
         l3 = s[name + "l3"]
         if scatter:
             piece = (up + uq) // nz
@@ -496,30 +553,6 @@
             push(fq.at[core], fq.at[core], at_core(), fq.at[1 - core]),
         ]
 
-    def write_tall(out, fp):
-        for h in range(2):
-            for r in range(0, 64, 8):
-                out[r * 16 : (r + 8) * 16, h * 128 : (h + 1) * 128] = fp[h, r : r + 8].astype(F32).reshape(128, 128)
-
-    def finish(name):
-        settle(progress[name])
-        fp, fq = s[name + "fp"], s[name + "fq"]
-        if name == "C":
-            write_tall(o_patch, fp)
-            for h in range(2):
-                at = slice(h * 128, (h + 1) * 128)
-                s["kg"][:, at] = fq[h, 0:7].astype(F32).reshape(112, 128)
-                s["eg"][:, at] = fq[h, 7:9].astype(F32).reshape(32, 128)
-            o_kernel[0] = s["kg"][0:49, :]
-            o_kernel[1] = s["kg"][49:98, :]
-            o_embed[...] = s["eg"][0 : OBSF + 1, :]
-            return
-        k = 1 if name == "A" else 0
-        write_tall(o_reduce.at[k], fp)
-        for lane in range(8):
-            part = fq[lane // 4, (lane % 4) * 16 : (lane % 4 + 1) * 16]
-            o_expand[k, :, lane * 128 : (lane + 1) * 128] = part.astype(F32).reshape(256, 128)
-
     def put_tall(name, left, right):
         for h in range(2):
             s[name + "gp"][h] = dot(left, right[:, h * 128 : (h + 1) * 128], TN).astype(BF16).reshape(64, 16, 128)
@@ -539,53 +572,91 @@
         put_tall(name, hidden, cotangent)
         put_wide(name, normed, grad_act)
         begin(name)
+        pad_inner(2 + k, grad_depth)
+        kernel_grad(k, grad_depth)
         if k == 0:
             stage_second("A")
-        pad_inner(2 + k, grad_depth)
-        kernel_grad(k, grad_depth, k * KSIDE * KSIDE)
+        stage_first(name)
         halo_wait(2 + k, copies)
-        cotangent = (cotangent.astype(F32) + convolve(2 + k, depth_k[k].astype(F32), True)).astype(BF16)
-        if k == 0:
-            stage_third("A")
-        stage_first(name)
+        cotangent = (cotangent.astype(F32) + convolve(2 + k, taps_of(k), True)).astype(BF16)
 
     parts = []
     for i in range(4):
         piece = normed_grid[i * CELLS : (i + 1) * CELLS]
         grad = dot(piece, cotangent, TN).astype(BF16)
         for h in range(2):
-            s["Cgp"][h, i * 16 : (i + 1) * 16] = grad[:, h * 128 : (h + 1) * 128].reshape(16, 16, 128)
+            target = s["Cgp"] if i < 2 else s["Cgq"]
+            target[h, (i % 2) * 16 : (i % 2 + 1) * 16] = grad[:, h * 128 : (h + 1) * 128].reshape(16, 16, 128)
         parts.append(dot(cotangent, patch_w[i * CH : (i + 1) * CH, :], NT))
     grad_grid = normalise_grad(grid_hat, grid_scale, jnp.concatenate(parts, axis=0)).astype(BF16)
     grad_embed = dot(encoded, grad_grid).astype(BF16)
-    grad_taps = s["kg"][...].astype(BF16)
+    for h in range(2):
+        s["Cgq"][h, 32:39] = s["kg"][h].astype(BF16).reshape(7, 16, 128)
+        s["Cgq"][h, 39:41] = grad_embed[:, h * 128 : (h + 1) * 128].reshape(2, 16, 128)
+        s["Cgq"][h, 41:48] = jnp.zeros((7, 16, 128), BF16)
+    begin("C")
+    stage_third("A")
+    stage_first("C")
+    stage_second("B")
+    stage_gather("A")
+    stage_second("C")
+    stage_third("B")
+    stage_back_second("A")
+    stage_third("C")
+    stage_gather("B")
+    stage_back_first("A")
+    stage_back_second("B")
+    stage_back_second("C")
+    stage_back_core("A")
+    stage_back_first("B")
+    stage_back_first("C")
+    stage_back_core("C")
+    stage_back_core("B")
+    for name in ("A", "C", "B"):
+        settle(progress[name])
+    for copy in sent:
+        copy.wait_send()
+
+
+def widen_kernel(feat, afp, afq, bfp, bfq, cfp, cfq, *refs):
+    outs, stage, rows, sems = refs[:6], refs[6:12], refs[12], refs[13]
+    s_feat, s_embed, s_patch, s_kernel, s_expand, s_reduce = stage
+    s_feat[...] = feat[...]
+    pending = []
+
+    def ship(src, dst):
+        copy = pltpu.make_async_copy(src, dst, sems.at[len(pending)])
+        copy.start()
+        pending.append(copy)
+
+    def block(units):
+        return units.astype(F32).reshape(units.shape[0] * 16, 128)
+
+    ship(s_feat, outs[0])
+    for k, fp, fq in ((1, afp, afq), (0, bfp, bfq)):
+        for r in range(0, 64, 16):
+            for h in range(2):
+                s_reduce[k, r * 16 : (r + 16) * 16, h * 128 : (h + 1) * 128] = block(fp[h, r : r + 16])
+        ship(s_reduce.at[k], outs[5].at[k])
+        for lane in range(8):
+            s_expand[k, :, lane * 128 : (lane + 1) * 128] = block(fq[lane // 4, (lane % 4) * 16 : (lane % 4 + 1) * 16])
+        ship(s_expand.at[k], outs[4].at[k])
+    for source, base in ((cfp, 0), (cfq, 512)):
+        for r in range(0, 32, 16):
+            for h in range(2):
+                at = slice(base + r * 16, base + (r + 16) * 16)
+                s_patch[at, h * 128 : (h + 1) * 128] = block(source[h, r : r + 16])
+    ship(s_patch, outs[2])
     for h in range(2):
         at = slice(h * 128, (h + 1) * 128)
-        s["Cgq"][h, 0:7] = grad_taps[:, at].reshape(7, 16, 128)
-        s["Cgq"][h, 7:9] = grad_embed[:, at].reshape(2, 16, 128)
-        s["Cgq"][h, 9:16] = jnp.zeros((7, 16, 128), BF16)
-    begin("C")
-    stage_gather("A")
-    stage_second("B")
-    stage_first("C")
-    stage_back_second("A")
-    stage_third("B")
-    stage_second("C")
-    stage_back_first("A")
-    stage_gather("B")
-    stage_third("C")
-    stage_back_core("A")
-    stage_back_second("B")
-    stage_back_second("C")
-    finish("A")
-    stage_back_first("B")
-    stage_back_first("C")
-    stage_back_core("B")
-    stage_back_core("C")
-    finish("B")
-    finish("C")
-    for copy in sent:
-        copy.wait_send()
+        rows[...] = block(cfq[h, 32:39])
+        for tap in range(KSIDE * KSIDE):
+            s_kernel[tap, :, at] = rows[2 * tap : 2 * tap + 2, :]
+        s_embed[:, at] = block(cfq[h, 39:41])[: OBSF + 1]
+    ship(s_kernel, outs[3])
+    ship(s_embed, outs[1])
+    for copy in pending:
+        copy.wait()
 
 
 def factor(lon):
@@ -602,25 +673,42 @@
     plan = scratch_plan(nx, ny, nz)
     copies = copy_count(nx, ny, nz)
     vmem = pl.BlockSpec(memory_space=pltpu.VMEM)
+    operands = (embed_w, patch_w, jnp.transpose(depth_k, (1, 0, 2)), expand_w, reduce_w, cot[0].reshape(CELLS, CH))
+    finals = []
+    for _, n_p, n_q, _ in GROUPS:
+        finals += [jax.ShapeDtypeStruct((2, n, 16, 128), BF16) for n in (n_p, n_q)]
+    handed = pl.pallas_call(
+        functools.partial(net_kernel, nx, ny, nz, tuple(plan)),
+        out_shape=(jax.ShapeDtypeStruct((CELLS, CH), BF16),) + tuple(finals),
+        in_specs=[vmem] * 2 + [pl.BlockSpec(memory_space=pltpu.HBM)] * 6,
+        out_specs=(vmem,) * 7,
+        scratch_shapes=list(plan.values())
+        + [pltpu.VMEM(leaf.shape, leaf.dtype) for leaf in operands]
+        + [pltpu.SemaphoreType.DMA((n,)) for n in (copies, copies, len(operands))],
+        compiler_params=pltpu.CompilerParams(
+            collective_id=0, has_side_effects=True, vmem_limit_bytes=32 * 2**20
+        ),
+    )(p0, p1, *(in_hbm(leaf) for leaf in operands))
+    shapes = (
+        jax.ShapeDtypeStruct((CELLS, CH), BF16),
+        jax.ShapeDtypeStruct((OBSF + 1, CH), F32),
+        jax.ShapeDtypeStruct((4 * CH, CH), F32),
+        jax.ShapeDtypeStruct((KSIDE * KSIDE, 2, CH), F32),
+        jax.ShapeDtypeStruct((2, CH, HID), F32),
+        jax.ShapeDtypeStruct((2, HID, CH), F32),
+    )
     outs = pl.pallas_call(
-        functools.partial(net_kernel, nx, ny, nz, tuple(plan)),
-        out_shape=(
-            jax.ShapeDtypeStruct((CELLS, CH), BF16),
-            jax.ShapeDtypeStruct((OBSF + 1, CH), F32),
-            jax.ShapeDtypeStruct((4 * CH, CH), F32),
-            jax.ShapeDtypeStruct((2, KSIDE * KSIDE, CH), F32),
-            jax.ShapeDtypeStruct((2, CH, HID), F32),
-            jax.ShapeDtypeStruct((2, HID, CH), F32),
-        ),
-        in_specs=[vmem] * 8,
-        out_specs=(vmem,) * 6,
-        scratch_shapes=list(plan.values())
-        + [pltpu.SemaphoreType.DMA((copies,)), pltpu.SemaphoreType.DMA((copies,))],
-        compiler_params=pltpu.CompilerParams(
-            collective_id=0, has_side_effects=True, vmem_limit_bytes=56 * 2**20
-        ),
-    )(p0, p1, embed_w, patch_w, depth_k, expand_w, reduce_w, cot[0].reshape(CELLS, CH))
-    return (outs[0].reshape(1, SIDE, SIDE, CH),) + tuple(outs[1:])
+        widen_kernel,
+        out_shape=shapes,
+        in_specs=[vmem] * 7,
+        out_specs=(pl.BlockSpec(memory_space=pltpu.HBM),) * 6,
+        scratch_shapes=[pltpu.VMEM(leaf.shape, leaf.dtype) for leaf in shapes]
+        + [pltpu.VMEM((112, 128), F32), pltpu.SemaphoreType.DMA((8,))],
+        compiler_params=pltpu.CompilerParams(vmem_limit_bytes=24 * 2**20),
+    )(*handed)
+    return (
+        outs[0].reshape(1, SIDE, SIDE, CH), outs[1], outs[2], jnp.transpose(outs[3], (1, 0, 2)), outs[4], outs[5],
+    )
 
 
 def solution(mesh):

time: 126 us -> 101 us (0.80)
  local copies, waits for them, and re-layouts: 16.9 us -> 0 us
  Pallas kernels: 108 us -> 100 us
    unnamed x23 -> x0, local copies, waits for them, and re-layouts: 16.9 us -> none
    pallas_call x1, Pallas kernels: 97.4 us -> 89.4 us  [on_device(): pl.pallas_call(functools.partial(net_kernel, nx, ny, nz, tuple(plan)), ou...]
    pallas_call x0 -> x1, Pallas kernels: none -> 2.5 us  [on_device(): pl.pallas_call(widen_kernel, out_shape=shapes, in_specs=[vmem] * 7, out_s...]
    pallas_call x1, Pallas kernels: 10.1 us -> 8.25 us  [encode(): pl.pallas_call(functools.partial(encode_kernel, nx, ny, nz), out_shape=(j...]
where the time goes in v2:
time: 101 us
  Pallas kernels  100 us (99%)
    pallas_call x1, Pallas kernels, on_device(): pl.pallas_call(functools.partial(net_kernel, nx, ny, nz, tuple(plan)), ou...  89.4 us
    pallas_call x1, Pallas kernels, encode(): pl.pallas_call(functools.partial(encode_kernel, nx, ny, nz), out_shape=(j...  8.25 us
    pallas_call x1, Pallas kernels, on_device(): pl.pallas_call(widen_kernel, out_shape=shapes, in_specs=[vmem] * 7, out_s...  2.5 us

profile of v2, /device:TPU:1, one launch (start us, length us, event | category | flops | bytes accessed | tf_op | source)
XLA Modules:
  0.0 100.8 jit_solution(18321408949769615134)
XLA Ops:
  0.6 8.2 %shard_map.145 = (bf16[144,16,128]{2,1,0:T(8,128)(2,1)S(1)}, bf16[128,16,128]{2,1,0:T(8,128)(2,1)S(1)}) custom-call(s32[64]{0:T(128)} %bitcast.12, s32[64]{0:T(128)} %bitcast.13, bf16[64,16,512]{2,1,0:T(8,128)(2,1)} %bitcast.8, f32[64,2,512]{2,1,0:T(2,128)} %bitcast.9), custom_call_target="tpu_custom_call" | custom-call | tf_op jit(solution)/shard_map/pallas_call | solution.py:109
  8.9 89.4 %shard_map.146 = (bf16[64,256]{1,0:T(8,128)(2,1)S(1)}, bf16[2,64,16,128]{3,2,1,0:T(8,128)(2,1)S(1)}, bf16[2,64,16,128]{3,2,1,0:T(8,128)(2,1)S(1)}, bf16[2,64,16,...) custom-call(bf16[144,16,128]{2,1,0:T(8,128)(2,1)S(1)} %get-tuple-ele, ...), custom_call_target="tpu_custom_call" | custom-call | tf_op jit(solution)/shard_map/pallas_call | solution.py:680
  98.3 2.5 %shard_map.147 = (bf16[64,256]{1,0:T(8,128)(2,1)}, f32[17,256]{1,0:T(8,128)}, f32[1024,256]{1,0:T(8,128)}, f32[49,2,256]{2,1,0:T(2,128)}, f32[2,256,1024]{2,1,0:T(8,128)}, /*index=5*/f32[2,1024,256]{2,1,0:T(8,128)}) custom-call(bf16[64,256]{1,0:T(8,128)(2,1)S(1)} %get-tuple-element.23.feat, bf16[2,64,16,128]{3,2,1,0:T(8,128)(2,1)S(1)} %get-tuple-element.24.afp, ...), custom_call_target="tpu_custom_call" | custom-call | tf_op jit(solution)/shard_map/pallas_call | solution.py:700

commit v3 on v2

--- a/solution.py
+++ b/solution.py
@@ -80,9 +80,12 @@
         for i in range(2):
             for j in range(2):
                 left = a[i * SIDE : (i + 1) * SIDE]
-                right = b[j * SIDE : (j + 1) * SIDE]
-                parts.append((left[:, None, :] * right[None]).reshape(CELLS, rows))
-        weight = jnp.concatenate(parts, axis=0).astype(BF16)
+                right = b[j * SIDE : (j + 1) * SIDE].astype(BF16)
+                right = jnp.concatenate([right, right], axis=0)
+                for p in range(0, SIDE, 2):
+                    pair_of = [jnp.broadcast_to(left[p + n : p + n + 1], (SIDE, rows)) for n in range(2)]
+                    parts.append(jnp.concatenate(pair_of, axis=0).astype(BF16) * right)
+        weight = jnp.concatenate(parts, axis=0)
         sums = dot(jnp.concatenate([values_ref[block], ones], axis=0), weight, NT)
         lon = tile // nz
         lat = tile % nz
@@ -99,7 +102,7 @@
     for part in range(parts):
         for copy in large[part]:
             copy.wait()
-        lax.fori_loop(part * share, (part + 1) * share, one_block, 0, unroll=min(share, 4))
+        lax.fori_loop(part * share, (part + 1) * share, one_block, 0, unroll=share)
     for lon in range(nx * ny):
         p0_ref[lon * (nz + 1) + nz] = dens_ref[lon].astype(BF16)
 
@@ -204,7 +207,7 @@
 def copy_count(nx, ny, nz):
     total = 2 * (nx + ny - 2) + (nz - 1) + 4 * 8
     for _, _, _, scatter in GROUPS:
-        total += 2 * 2 + 4 * (nx + ny - 2) + (nz - 1) * (2 if scatter else 1)
+        total += 2 * (nx + ny) + 4 * (nx + ny - 2) + (nz - 1) * (2 if scatter else 1)
     return total
 
 
@@ -445,37 +448,52 @@
     def group(name):
         return next(entry for entry in GROUPS if entry[0] == name)
 
+    def lines(name):
+        _, n_p, n_q, _ = group(name)
+        return (("p", n_p, nx, x, at_x, ny, y, at_y), ("q", n_q, ny, y, at_y, nx, x, at_x))
+
     def begin(name):
-        gp, gq = s[name + "gp"], s[name + "gq"]
-        progress[name] = [
-            push(gp.at[1 - core], s[name + "cp"], at_core()),
-            push(gq.at[1 - core], s[name + "cq"], at_core()),
-        ]
+        found = []
+        for d in [*range(1, max(nx, ny)), 0]:
+            for key, n, count, place, _, _, _, _ in lines(name):
+                if d < count:
+                    size = n // count
+                    at = pl.ds(((place + d) % count) * size, size)
+                    found.append((key, d, push(s[name + "g" + key].at[1 - core, at], s[name + "c" + key].at[at], at_core())))
+        progress[name] = found
 
     def stage_first(name):
-        _, n_p, n_q, _ = group(name)
+        found = []
+        info = {line[0]: line for line in lines(name)}
+        for key, d, copy in progress[name]:
+            _, n, count, place, where, _, _, _ = info[key]
+            size = n // count
+            copy.wait_recv()
+            own, got, out = s[name + "g" + key], s[name + "c" + key], s[name + "s" + key]
+            base = ((place + d) % count) * size
+            step = math.gcd(8, size)
+            for i in range(0, size, step):
+                at = pl.ds(base + i, step)
+                out[at] = (own[core, at].astype(F32) + got[at].astype(F32)).astype(BF16)
+            if d:
+                found.append(push(out.at[pl.ds(base, size)], s[name + "l1" + key].at[d - 1], where(d)))
+        progress[name] = found
+
+    def stage_second(name):
         settle(progress[name])
-        for key, n in (("p", n_p), ("q", n_q)):
-            own, got, out = s[name + "g" + key], s[name + "c" + key], s[name + "s" + key]
-
-            def body(i, carry, own=own, got=got, out=out):
-                at = pl.ds(pl.multiple_of(i * 8, 8), 8)
-                out[at] = (own[core, at].astype(F32) + got[at].astype(F32)).astype(BF16)
-                return carry
-
-            lax.fori_loop(0, n // 8, body, 0)
-        progress[name] = spread(s[name + "sp"], s[name + "l1p"], n_p // nx, nx, "x") + spread(
-            s[name + "sq"], s[name + "l1q"], n_q // ny, ny, "y"
-        )
-
-    def stage_second(name):
-        _, n_p, n_q, _ = group(name)
-        settle(progress[name])
-        fold(s[name + "s2p"], s[name + "sp"], s[name + "l1p"], nx, x * (n_p // nx), n_p // nx, math.gcd(8, n_p // nx))
-        fold(s[name + "s2q"], s[name + "sq"], s[name + "l1q"], ny, y * (n_q // ny), n_q // ny, math.gcd(8, n_q // ny))
-        progress[name] = spread(s[name + "s2p"], s[name + "l2p"], n_p // nlon, ny, "y") + spread(
-            s[name + "s2q"], s[name + "l2q"], n_q // nlon, nx, "x"
-        )
+        found = []
+        for key, n, first, place, _, second, place_2, where in lines(name):
+            size, small = n // first, n // (first * second)
+            own, land, out = s[name + "s" + key], s[name + "l1" + key], s[name + "s2" + key]
+            for d in [*range(1, second), 0]:
+                base = ((place_2 + d) % second) * small
+                total = own[pl.ds(place * size + base, small)].astype(F32)
+                for e in range(first - 1):
+                    total = total + land[e, pl.ds(base, small)].astype(F32)
+                out[pl.ds(base, small)] = total.astype(BF16)
+                if d:
+                    found.append(push(out.at[pl.ds(base, small)], s[name + "l2" + key].at[d - 1], where(d)))
+        progress[name] = found
 
     def stage_third(name):
         _, n_p, n_q, scatter = group(name)
@@ -531,27 +549,34 @@
         progress[name] += [push(from_q(0), from_q(0), at_x(d), from_q(d)) for d in range(1, nx)]
 
     def stage_back_first(name):
-        _, n_p, n_q, _ = group(name)
         settle(progress[name])
-        fp, fq = s[name + "fp"], s[name + "fq"]
-        hp, hq = n_p // nx, n_q // ny
-
-        def from_p(d):
-            return fp.at[core, pl.ds(((x + nx - d) % nx) * hp, hp)]
-
-        def from_q(d):
-            return fq.at[core, pl.ds(((y + ny - d) % ny) * hq, hq)]
-
-        progress[name] = [push(from_p(0), from_p(0), at_x(d), from_p(d)) for d in range(1, nx)]
-        progress[name] += [push(from_q(0), from_q(0), at_y(d), from_q(d)) for d in range(1, ny)]
+        found, handed = [], []
+        for d in range(0, max(nx, ny)):
+            for key, n, count, place, where, _, _, _ in lines(name):
+                if d >= count:
+                    continue
+                size, whole = n // count, s[name + "f" + key]
+                own = whole.at[core, pl.ds(place * size, size)]
+                at = pl.ds(((place + count - d) % count) * size, size)
+                if d:
+                    found.append((whole, at, push(own, own, where(d), whole.at[core, at])))
+                else:
+                    handed.append((whole, at))
+        hand_over(name, handed)
+        progress[name] = (found, progress[name])
+
+    def hand_over(name, handed):
+        progress[name] = [
+            push(whole.at[core, at], whole.at[core, at], at_core(), whole.at[1 - core, at]) for whole, at in handed
+        ]
 
     def stage_back_core(name):
-        settle(progress[name])
-        fp, fq = s[name + "fp"], s[name + "fq"]
-        progress[name] = [
-            push(fp.at[core], fp.at[core], at_core(), fp.at[1 - core]),
-            push(fq.at[core], fq.at[core], at_core(), fq.at[1 - core]),
-        ]
+        found, earlier = progress[name]
+        for whole, at, copy in found:
+            copy.wait_recv()
+            hand_over(name, [(whole, at)])
+            earlier = earlier + progress[name]
+        progress[name] = earlier
 
     def put_tall(name, left, right):
         for h in range(2):

time: 101 us -> 98.8 us (0.978)
  Pallas kernels: 100 us -> 98 us
    pallas_call x1, Pallas kernels: 8.25 us -> 6.48 us  [encode(): pl.pallas_call(functools.partial(encode_kernel, nx, ny, nz), out_shape=(j...]
where the time goes in v3:
time: 98.8 us; the launch traced here: 98.7 us
  Pallas kernels  98 us (99%)
    pallas_call x1, Pallas kernels, on_device(): pl.pallas_call(functools.partial(net_kernel, nx, ny, nz, tuple(plan)), ou...  89 us
    pallas_call x1, Pallas kernels, encode(): pl.pallas_call(functools.partial(encode_kernel, nx, ny, nz), out_shape=(j...  6.48 us
    pallas_call x1, Pallas kernels, on_device(): pl.pallas_call(widen_kernel, out_shape=shapes, in_specs=[vmem] * 7, out_s...  2.5 us

profile of v3, /device:TPU:1, one launch (start us, length us, event | category | flops | bytes accessed | tf_op | source)
XLA Modules:
  0.0 98.7 jit_solution(16137090233718635992)
XLA Ops:
  0.6 6.5 %shard_map.145 = (bf16[144,16,128]{2,1,0:T(8,128)(2,1)S(1)}, bf16[128,16,128]{2,1,0:T(8,128)(2,1)S(1)}) custom-call(s32[64]{0:T(128)} %bitcast.12, s32[64]{0:T(128)} %bitcast.13, bf16[64,16,512]{2,1,0:T(8,128)(2,1)} %bitcast.8, f32[64,2,512]{2,1,0:T(2,128)} %bitcast.9), custom_call_target="tpu_custom_call" | custom-call | tf_op jit(solution)/shard_map/pallas_call | solution.py:112
  7.1 89.0 %shard_map.146 = (bf16[64,256]{1,0:T(8,128)(2,1)S(1)}, bf16[2,64,16,128]{3,2,1,0:T(8,128)(2,1)S(1)}, bf16[2,64,16,128]{3,2,1,0:T(8,128)(2,1)S(1)}, bf16[2,64,16,...) custom-call(bf16[144,16,128]{2,1,0:T(8,128)(2,1)S(1)} %get-tuple-ele, ...), custom_call_target="tpu_custom_call" | custom-call | tf_op jit(solution)/shard_map/pallas_call | solution.py:705
  96.2 2.5 %shard_map.147 = (bf16[64,256]{1,0:T(8,128)(2,1)}, f32[17,256]{1,0:T(8,128)}, f32[1024,256]{1,0:T(8,128)}, f32[49,2,256]{2,1,0:T(2,128)}, f32[2,256,1024]{2,1,0:T(8,128)}, /*index=5*/f32[2,1024,256]{2,1,0:T(8,128)}) custom-call(bf16[64,256]{1,0:T(8,128)(2,1)S(1)} %get-tuple-element.23.feat, bf16[2,64,16,128]{3,2,1,0:T(8,128)(2,1)S(1)} %get-tuple-element.24.afp, ...), custom_call_target="tpu_custom_call" | custom-call | tf_op jit(solution)/shard_map/pallas_call | solution.py:725

commit v4 on v3

--- a/solution.py
+++ b/solution.py
@@ -30,103 +30,56 @@
 
 
 PARTS = 4
+SLOTS = 128
 
 
 def in_hbm(array):
     return pltpu.with_memory_space_constraint(array, pltpu.HBM)
 
 
-def encode_kernel(
-    nx, ny, nz, dest_hbm, count_hbm, values_hbm, coords_hbm, p0_ref, p1_ref, dens_ref,
-    dest_ref, count_ref, values_ref, coords_ref, sems,
-):
-    blocks = values_ref.shape[0]
-    parts = PARTS if blocks % PARTS == 0 else 1
-    share = blocks // parts
-    small = [
-        pltpu.make_async_copy(dest_hbm, dest_ref, sems.at[0]),
-        pltpu.make_async_copy(count_hbm, count_ref, sems.at[1]),
-    ]
-    large = []
-    for part in range(parts):
-        at = pl.ds(part * share, share)
-        large.append(
-            (
-                pltpu.make_async_copy(values_hbm.at[at], values_ref.at[at], sems.at[2 + 2 * part]),
-                pltpu.make_async_copy(coords_hbm.at[at], coords_ref.at[at], sems.at[3 + 2 * part]),
-            )
-        )
-    for copy in small:
-        copy.start()
-    for pair in large:
-        for copy in pair:
-            copy.start()
-    p0_ref[...] = jnp.zeros_like(p0_ref)
-    p1_ref[...] = jnp.zeros_like(p1_ref)
-    dens_ref[...] = jnp.zeros_like(dens_ref)
+def encode_block(block, count_ref, values_ref, coords_ref):
     rows = values_ref.shape[2]
     order = lax.broadcasted_iota(jnp.int32, (TILE, rows), 0)
     cell = (2 * (order % SIDE) + order // SIDE).astype(F32)
     lane = lax.broadcasted_iota(jnp.int32, (TILE, rows), 1)
+    pair = coords_ref[block]
+    a = jnp.exp(-jnp.square(pair[0:1, :] - cell) * INVERSE)
+    a = jnp.where(lane < count_ref[block], a, 0.0)
+    b = jnp.exp(-jnp.square(pair[1:2, :] - cell) * INVERSE)
+    parts = []
+    for i in range(2):
+        for j in range(2):
+            left = a[i * SIDE : (i + 1) * SIDE]
+            right = b[j * SIDE : (j + 1) * SIDE].astype(BF16)
+            right = jnp.concatenate([right, right], axis=0)
+            for p in range(0, SIDE, 2):
+                pair_of = [jnp.broadcast_to(left[p + n : p + n + 1], (SIDE, rows)) for n in range(2)]
+                parts.append(jnp.concatenate(pair_of, axis=0).astype(BF16) * right)
+    weight = jnp.concatenate(parts, axis=0)
     ones = jnp.ones((OBSF, rows), BF16)
-
-    def one_block(block, carry):
-        tile = dest_ref[block]
-        pair = coords_ref[block]
-        a = jnp.exp(-jnp.square(pair[0:1, :] - cell) * INVERSE)
-        a = jnp.where(lane < count_ref[block], a, 0.0)
-        b = jnp.exp(-jnp.square(pair[1:2, :] - cell) * INVERSE)
-        parts = []
-        for i in range(2):
-            for j in range(2):
-                left = a[i * SIDE : (i + 1) * SIDE]
-                right = b[j * SIDE : (j + 1) * SIDE].astype(BF16)
-                right = jnp.concatenate([right, right], axis=0)
-                for p in range(0, SIDE, 2):
-                    pair_of = [jnp.broadcast_to(left[p + n : p + n + 1], (SIDE, rows)) for n in range(2)]
-                    parts.append(jnp.concatenate(pair_of, axis=0).astype(BF16) * right)
-        weight = jnp.concatenate(parts, axis=0)
-        sums = dot(jnp.concatenate([values_ref[block], ones], axis=0), weight, NT)
-        lon = tile // nz
-        lat = tile % nz
-        x = lon // ny
-        y = lon % ny
-        p0_ref[lon * (nz + 1) + lat] = sums[:OBSF, :128].astype(BF16)
-        p1_ref[(y * nx + x) * nz + lat] = sums[:OBSF, 128:].astype(BF16)
-        dens_ref[lon, pl.ds(lat, 1), :] = sums[OBSF : OBSF + 1, :128]
-        dens_ref[lon, pl.ds(SIDE + lat, 1), :] = sums[OBSF : OBSF + 1, 128:]
+    return dot(jnp.concatenate([values_ref[block], ones], axis=0), weight, NT)
+
+
+def encode_part(part, share, count_ref, values_ref, coords_ref, res0, res1, resd):
+    def body(block, carry):
+        sums = encode_block(block, count_ref, values_ref, coords_ref)
+        res0[block + 1] = sums[:OBSF, :128].astype(BF16)
+        res1[block + 1] = sums[:OBSF, 128:].astype(BF16)
+        resd[block + 1, 0:1, :] = sums[OBSF : OBSF + 1, :128]
+        resd[block + 1, 1:2, :] = sums[OBSF : OBSF + 1, 128:]
         return carry
 
-    for copy in small:
-        copy.wait()
-    for part in range(parts):
-        for copy in large[part]:
-            copy.wait()
-        lax.fori_loop(part * share, (part + 1) * share, one_block, 0, unroll=share)
-    for lon in range(nx * ny):
-        p0_ref[lon * (nz + 1) + nz] = dens_ref[lon].astype(BF16)
-
-
-def encode(nx, ny, nz, dest, count, values, coords):
-    lon = nx * ny
-    return pl.pallas_call(
-        functools.partial(encode_kernel, nx, ny, nz),
-        out_shape=(
-            jax.ShapeDtypeStruct((lon * (nz + 1), 16, 128), BF16),
-            jax.ShapeDtypeStruct((lon * nz, 16, 128), BF16),
-        ),
-        in_specs=[pl.BlockSpec(memory_space=pltpu.HBM)] * 4,
-        out_specs=(pl.BlockSpec(memory_space=pltpu.VMEM),) * 2,
-        scratch_shapes=[
-            pltpu.VMEM((lon, 16, 128), F32),
-            pltpu.SMEM(dest.shape, jnp.int32),
-            pltpu.SMEM(count.shape, jnp.int32),
-            pltpu.VMEM(values.shape, values.dtype),
-            pltpu.VMEM(coords.shape, coords.dtype),
-            pltpu.SemaphoreType.DMA((2 + 2 * PARTS,)),
-        ],
-        compiler_params=pltpu.CompilerParams(vmem_limit_bytes=24 * 2**20),
-    )(*(in_hbm(leaf) for leaf in (dest, count, values, coords)))
+    lax.fori_loop(part * share, (part + 1) * share, body, 0, unroll=share)
+
+
+def slot_of_tile(dest, blocks):
+    row = lax.broadcasted_iota(jnp.int32, (blocks, blocks), 0)
+    column = lax.broadcasted_iota(jnp.int32, (blocks, blocks), 1)
+    spread = jnp.where(row == column, jnp.broadcast_to(dest, (blocks, blocks)), 0)
+    upright = jnp.sum(spread, axis=1, keepdims=True)
+    tile = lax.broadcasted_iota(jnp.int32, (blocks, SLOTS), 1)
+    number = lax.broadcasted_iota(jnp.int32, (blocks, SLOTS), 0) + 1
+    return jnp.minimum(jnp.sum(jnp.where(upright == tile, number, 0), axis=0, keepdims=True), blocks)
 
 
 def normalise(field):
@@ -179,11 +132,19 @@
 GROUPS = (("A", 64, 64, True), ("B", 64, 64, True), ("C", 32, 48, False))
 
 
-def scratch_plan(nx, ny, nz):
+def scratch_plan(nx, ny, nz, blocks):
     def units(*lead):
         return pltpu.VMEM(tuple(lead) + (16, 128), BF16)
 
+    lon = nx * ny
     plan = {
+        "p0": units(lon * (nz + 1)), "p1": units(lon * nz),
+        "res0": units(blocks + 1), "res1": units(blocks + 1),
+        "resd": pltpu.VMEM((blocks + 1, 2, 128), F32),
+        "densities": pltpu.VMEM((lon, 16, 128), F32),
+        "slots_v": pltpu.VMEM((1, SLOTS), jnp.int32),
+        "slots": pltpu.SMEM((1, SLOTS), jnp.int32),
+        "corner": pltpu.VMEM((16, CH), F32),
         "r0": units(nx - 1, ny * (nz + 1)), "r1": units(ny - 1, nx * nz),
         "q0": units(ny * (nz + 1)), "q1": units(nx * nz),
         "t0": units(ny - 1, nz + 1), "t1": units(nx - 1, nz),
@@ -195,6 +156,7 @@
     }
     for k in range(4):
         plan["halo_src%d" % k] = pltpu.VMEM((2, CELLS, CH), BF16)
+        plan["halo_corner%d" % k] = pltpu.VMEM((4, 16, CH), BF16)
         plan["halo_dst%d" % k] = pltpu.VMEM((8, CELLS // 2, CH), BF16)
         plan["pad%d" % k] = pltpu.VMEM((2, 14 * PADW, 128), F32)
     plan["cols"] = pltpu.VMEM((CELLS, CH), F32)
@@ -211,21 +173,39 @@
     return total
 
 
+INPUTS = 10
 FINALS = ("Afp", "Afq", "Bfp", "Bfq", "Cfp", "Cfq")
 HALOS = tuple((i, j) for i in (-1, 0, 1) for j in (-1, 0, 1) if (i, j) != (0, 0))
 
 
 def net_kernel(nx, ny, nz, names, *refs):
-    p0, p1 = refs[:2]
-    feat = refs[8]
-    s = dict(zip(FINALS, refs[9:15]))
-    s.update(zip(names, refs[15:]))
-    local = refs[15 + len(names) : 21 + len(names)]
-    embed_w, patch_w, depth_k, expand_w, reduce_w, cot = local
-    send_sem, recv_sem, load_sem = refs[21 + len(names) :]
+    far, feat, rest = refs[:INPUTS], refs[INPUTS], refs[INPUTS + 1 :]
+    s = dict(zip(FINALS, rest[: len(FINALS)]))
+    rest = rest[len(FINALS) :]
+    s.update(zip(names, rest))
+    rest = rest[len(names) :]
+    near = rest[:INPUTS]
+    dest_ref, count_ref, values_ref, coords_ref, embed_w, patch_w, depth_k, expand_w, reduce_w, cot = near
+    send_sem, recv_sem, load_sem = rest[INPUTS:]
+    blocks = values_ref.shape[0]
+    parts = PARTS if blocks % PARTS == 0 else 1
+    share = blocks // parts
+    first_loads = [pltpu.make_async_copy(far[i], near[i], load_sem.at[i]) for i in range(2)]
+    block_loads = []
+    for part in range(parts):
+        at = pl.ds(part * share, share)
+        block_loads.append(
+            [
+                pltpu.make_async_copy(far[i].at[at], near[i].at[at], load_sem.at[i + 2 * part])
+                for i in (2, 3)
+            ]
+        )
     loads = [
-        pltpu.make_async_copy(far, near, load_sem.at[i]) for i, (far, near) in enumerate(zip(refs[2:8], local))
+        pltpu.make_async_copy(far[i], near[i], load_sem.at[i + 2 * PARTS]) for i in range(4, INPUTS)
     ]
+    slot_load = pltpu.make_async_copy(s["slots_v"], s["slots"], load_sem.at[INPUTS + 2 * PARTS])
+    for load in first_loads + [load for part in block_loads for load in part]:
+        load.start()
     core = lax.axis_index("dp")
     lon = lax.axis_index("lon")
     z = lax.axis_index("lat")
@@ -253,6 +233,39 @@
     peers += [at_z(d) for d in range(1, nz)] + [at_halo(i, j) for i, j in HALOS]
     for peer in peers:
         pl.semaphore_signal(barrier, inc=1, device_id=peer, device_id_type=MESH)
+    for load in loads:
+        load.start()
+
+    for load in first_loads:
+        load.wait()
+    s["slots_v"][...] = slot_of_tile(dest_ref[...], blocks)
+    slot_load.start()
+    res0, res1, resd = s["res0"], s["res1"], s["resd"]
+    res0[0] = jnp.zeros((16, 128), BF16)
+    res1[0] = jnp.zeros((16, 128), BF16)
+    resd[0] = jnp.zeros((2, 128), F32)
+    for part in range(parts):
+        for load in block_loads[part]:
+            load.wait()
+        encode_part(part, share, count_ref, values_ref, coords_ref, res0, res1, resd)
+    slot_load.wait()
+    p0, p1, densities = s["p0"], s["p1"], s["densities"]
+
+    def fill(tile_lon, carry):
+        tile_x, tile_y = tile_lon // ny, tile_lon % ny
+        for tile_z in range(nz):
+            slot = jnp.clip(s["slots"][0, tile_lon * nz + tile_z], 0, blocks)
+            p0[tile_lon * (nz + 1) + tile_z] = res0[slot]
+            p1[(tile_y * nx + tile_x) * nz + tile_z] = res1[slot]
+            density = resd[slot]
+            densities[tile_lon, tile_z : tile_z + 1, :] = density[0:1]
+            densities[tile_lon, SIDE + tile_z : SIDE + tile_z + 1, :] = density[1:2]
+        p0[tile_lon * (nz + 1) + nz] = densities[tile_lon].astype(BF16)
+        return carry
+
+    if nz < SIDE:
+        densities[...] = jnp.zeros_like(densities)
+    lax.fori_loop(0, nlon, fill, 0, unroll=2)
     pl.semaphore_wait(barrier, len(peers))
 
     sent = []
@@ -292,8 +305,6 @@
 
     w0, w1 = nz + 1, nz
     copies = spread(p0, s["r0"], ny * w0, nx, "x") + spread(p1, s["r1"], nx * w1, ny, "y")
-    for load in loads:
-        load.start()
     s["ew"][...] = jnp.zeros_like(s["ew"])
     for load in loads:
         load.wait()
@@ -341,14 +352,24 @@
     def halo_send(which, field):
         src, dst = s["halo_src%d" % which], s["halo_dst%d" % which]
         src[0] = field.astype(BF16)
-        src[1] = jnp.swapaxes(field.reshape(SIDE, SIDE, CH), 0, 1).reshape(CELLS, CH).astype(BF16)
+        turned = jnp.swapaxes(field.reshape(SIDE, SIDE, CH), 0, 1)
+        src[1] = turned.reshape(CELLS, CH).astype(BF16)
+        corner, corners = s["corner"], s["halo_corner%d" % which]
         found = []
         for index, (i, j) in enumerate(HALOS):
             if j == 0:
                 piece = src.at[0, pl.ds(32 if i > 0 else 0, 32)]
+                found.append(push(piece, dst.at[index], at_halo(i, j)))
+            elif i == 0:
+                piece = src.at[1, pl.ds(32 if j > 0 else 0, 32)]
+                found.append(push(piece, dst.at[index], at_halo(i, j)))
             else:
-                piece = src.at[1, pl.ds(32 if j > 0 else 0, 32)]
-            found.append(push(piece, dst.at[index], at_halo(i, j)))
+                for r in range(4):
+                    q, p = (4 if j > 0 else 0) + r, 4 if i > 0 else 0
+                    corner[r * 4 : r * 4 + 4, :] = turned[q][p : p + 4]
+                slot = (i > 0) * 2 + (j > 0)
+                corners[slot] = corner[...].astype(BF16)
+                found.append(push(corners.at[slot], dst.at[index, pl.ds(0, 16)], at_halo(i, j)))
         return found
 
     def pad_inner(which, field):
@@ -376,19 +397,18 @@
                 continue
             inside = (z > 0) if j > 0 else (z < nz - 1)
             keep = jnp.where(inside, 1.0, 0.0).astype(F32)
-            block = dst[index].astype(F32) * keep
+            block = (dst[index] if i == 0 else dst[index, 0:16, :]).astype(F32) * keep
             for r in range(REACH):
                 if j > 0:
                     column, at = r, 1 + r
                 else:
                     column, at = REACH + SIDE + r, r
-                strip = block[at * SIDE : (at + 1) * SIDE]
                 if i == 0:
-                    top, strip = REACH, strip
+                    top, strip = REACH, block[at * SIDE : (at + 1) * SIDE]
                 elif i > 0:
-                    top, strip = 0, strip[SIDE - REACH :]
+                    top, strip = 0, block[at * 4 + 1 : at * 4 + 4]
                 else:
-                    top, strip = REACH + SIDE, strip[:REACH]
+                    top, strip = REACH + SIDE, block[at * 4 : at * 4 + REACH]
                 for h in range(2):
                     pad[h, pl.ds(top * PADW + column, strip.shape[0], PADW), :] = strip[:, h * 128 : (h + 1) * 128]
 
@@ -604,6 +624,7 @@
         stage_first(name)
         halo_wait(2 + k, copies)
         cotangent = (cotangent.astype(F32) + convolve(2 + k, taps_of(k), True)).astype(BF16)
+    stage_third("A")
 
     parts = []
     for i in range(4):
@@ -620,7 +641,6 @@
         s["Cgq"][h, 39:41] = grad_embed[:, h * 128 : (h + 1) * 128].reshape(2, 16, 128)
         s["Cgq"][h, 41:48] = jnp.zeros((7, 16, 128), BF16)
     begin("C")
-    stage_third("A")
     stage_first("C")
     stage_second("B")
     stage_gather("A")
@@ -694,26 +714,28 @@
 def on_device(values, coords, dest, count, embed_w, patch_w, depth_k, expand_w, reduce_w, cot):
     nx, ny = factor(lax.axis_size("lon"))
     nz = lax.axis_size("lat")
-    p0, p1 = encode(nx, ny, nz, dest[0, 0, 0], count[0, 0, 0], values[0, 0, 0], coords[0, 0, 0])
-    plan = scratch_plan(nx, ny, nz)
+    operands = (
+        dest[0, 0], count[0, 0, 0], values[0, 0, 0], coords[0, 0, 0],
+        embed_w, patch_w, jnp.transpose(depth_k, (1, 0, 2)), expand_w, reduce_w, cot[0].reshape(CELLS, CH),
+    )
+    plan = scratch_plan(nx, ny, nz, values.shape[3])
     copies = copy_count(nx, ny, nz)
     vmem = pl.BlockSpec(memory_space=pltpu.VMEM)
-    operands = (embed_w, patch_w, jnp.transpose(depth_k, (1, 0, 2)), expand_w, reduce_w, cot[0].reshape(CELLS, CH))
     finals = []
     for _, n_p, n_q, _ in GROUPS:
         finals += [jax.ShapeDtypeStruct((2, n, 16, 128), BF16) for n in (n_p, n_q)]
     handed = pl.pallas_call(
         functools.partial(net_kernel, nx, ny, nz, tuple(plan)),
         out_shape=(jax.ShapeDtypeStruct((CELLS, CH), BF16),) + tuple(finals),
-        in_specs=[vmem] * 2 + [pl.BlockSpec(memory_space=pltpu.HBM)] * 6,
+        in_specs=[pl.BlockSpec(memory_space=pltpu.HBM)] * INPUTS,
         out_specs=(vmem,) * 7,
         scratch_shapes=list(plan.values())
-        + [pltpu.VMEM(leaf.shape, leaf.dtype) for leaf in operands]
-        + [pltpu.SemaphoreType.DMA((n,)) for n in (copies, copies, len(operands))],
+        + [(pltpu.SMEM if i == 1 else pltpu.VMEM)(leaf.shape, leaf.dtype) for i, leaf in enumerate(operands)]
+        + [pltpu.SemaphoreType.DMA((n,)) for n in (copies, copies, INPUTS + 2 * PARTS + 1)],
         compiler_params=pltpu.CompilerParams(
             collective_id=0, has_side_effects=True, vmem_limit_bytes=32 * 2**20
         ),
-    )(p0, p1, *(in_hbm(leaf) for leaf in operands))
+    )(*(in_hbm(leaf) for leaf in operands))
     shapes = (
         jax.ShapeDtypeStruct((CELLS, CH), BF16),
         jax.ShapeDtypeStruct((OBSF + 1, CH), F32),

time: 98.8 us -> 95.3 us (0.965)
  Pallas kernels: 98 us -> 94.4 us
    pallas_call x1 -> x0, Pallas kernels: 6.48 us -> none  [encode(): pl.pallas_call(functools.partial(encode_kernel, nx, ny, nz), out_shape=(j...]
    pallas_call x1, Pallas kernels: 89 us -> 91.9 us  [on_device(): pl.pallas_call(functools.partial(net_kernel, nx, ny, nz, tuple(plan)), ou...]
where the time goes in v4:
time: 95.3 us; the launch traced here: 95.2 us
  Pallas kernels  94.4 us (99%)
    pallas_call x1, Pallas kernels, on_device(): pl.pallas_call(functools.partial(net_kernel, nx, ny, nz, tuple(plan)), ou...  91.9 us
    pallas_call x1, Pallas kernels, on_device(): pl.pallas_call(widen_kernel, out_shape=shapes, in_specs=[vmem] * 7, out_s...  2.5 us

profile of v4, /device:TPU:1, one launch (start us, length us, event | category | flops | bytes accessed | tf_op | source)
XLA Modules:
  0.0 95.2 jit_solution(15861180992618730501)
XLA Ops:
  0.6 91.9 %shard_map.145 = (bf16[64,256]{1,0:T(8,128)(2,1)S(1)}, bf16[2,64,16,128]{3,2,1,0:T(8,128)(2,1)S(1)}, bf16[2,64,16,128]{3,2,1,0:T(8,128)(2,1)S(1)}, bf16[2,64,16,...) custom-call(s32[1,64]{1,0:T(1,128)} %bitcast.12, ...), custom_call_target="tpu_custom_call" | custom-call | tf_op jit(solution)/shard_map/pallas_call | solution.py:727
  92.5 2.5 %shard_map.146 = (bf16[64,256]{1,0:T(8,128)(2,1)}, f32[17,256]{1,0:T(8,128)}, f32[1024,256]{1,0:T(8,128)}, f32[49,2,256]{2,1,0:T(2,128)}, f32[2,256,1024]{2,1,0:T(8,128)}, /*index=5*/f32[2,1024,256]{2,1,0:T(8,128)}) custom-call(bf16[64,256]{1,0:T(8,128)(2,1)S(1)} %get-tuple-element.19.feat, bf16[2,64,16,128]{3,2,1,0:T(8,128)(2,1)S(1)} %get-tuple-element.20.afp, ...), custom_call_target="tpu_custom_call" | custom-call | tf_op jit(solution)/shard_map/pallas_call | solution.py:747

commit v5 on v4

--- a/solution.py
+++ b/solution.py
@@ -625,6 +625,7 @@
         halo_wait(2 + k, copies)
         cotangent = (cotangent.astype(F32) + convolve(2 + k, taps_of(k), True)).astype(BF16)
     stage_third("A")
+    stage_second("B")
 
     parts = []
     for i in range(4):
@@ -642,21 +643,20 @@
         s["Cgq"][h, 41:48] = jnp.zeros((7, 16, 128), BF16)
     begin("C")
     stage_first("C")
-    stage_second("B")
+    stage_third("B")
     stage_gather("A")
     stage_second("C")
-    stage_third("B")
     stage_back_second("A")
+    stage_gather("B")
     stage_third("C")
-    stage_gather("B")
     stage_back_first("A")
     stage_back_second("B")
     stage_back_second("C")
-    stage_back_core("A")
     stage_back_first("B")
     stage_back_first("C")
+    stage_back_core("A")
+    stage_back_core("B")
     stage_back_core("C")
-    stage_back_core("B")
     for name in ("A", "C", "B"):
         settle(progress[name])
     for copy in sent:

time: 95.3 us -> 93.9 us (0.985)
  Pallas kernels: 94.4 us -> 93 us
    pallas_call x1, Pallas kernels: 91.9 us -> 90.5 us  [on_device(): pl.pallas_call(functools.partial(net_kernel, nx, ny, nz, tuple(plan)), ou...]
where the time goes in v5:
time: 93.9 us; the launch traced here: 93.8 us
  Pallas kernels  93 us (99%)
    pallas_call x1, Pallas kernels, on_device(): pl.pallas_call(functools.partial(net_kernel, nx, ny, nz, tuple(plan)), ou...  90.5 us
    pallas_call x1, Pallas kernels, on_device(): pl.pallas_call(widen_kernel, out_shape=shapes, in_specs=[vmem] * 7, out_s...  2.5 us

profile of v5, /device:TPU:1, one launch (start us, length us, event | category | flops | bytes accessed | tf_op | source)
XLA Modules:
  0.0 93.8 jit_solution(17429570989535337740)
XLA Ops:
  0.6 90.5 %shard_map.145 = (bf16[64,256]{1,0:T(8,128)(2,1)S(1)}, bf16[2,64,16,128]{3,2,1,0:T(8,128)(2,1)S(1)}, bf16[2,64,16,128]{3,2,1,0:T(8,128)(2,1)S(1)}, bf16[2,64,16,...) custom-call(s32[1,64]{1,0:T(1,128)} %bitcast.12, ...), custom_call_target="tpu_custom_call" | custom-call | tf_op jit(solution)/shard_map/pallas_call | solution.py:727
  91.2 2.5 %shard_map.146 = (bf16[64,256]{1,0:T(8,128)(2,1)}, f32[17,256]{1,0:T(8,128)}, f32[1024,256]{1,0:T(8,128)}, f32[49,2,256]{2,1,0:T(2,128)}, f32[2,256,1024]{2,1,0:T(8,128)}, /*index=5*/f32[2,1024,256]{2,1,0:T(8,128)}) custom-call(bf16[64,256]{1,0:T(8,128)(2,1)S(1)} %get-tuple-element.19.feat, bf16[2,64,16,128]{3,2,1,0:T(8,128)(2,1)S(1)} %get-tuple-element.20.afp, ...), custom_call_target="tpu_custom_call" | custom-call | tf_op jit(solution)/shard_map/pallas_call | solution.py:747

commit v6 on v5

--- a/solution.py
+++ b/solution.py
@@ -614,17 +614,18 @@
         grad_act = (dot(cotangent, reduce_w[k], NT) * slope).astype(BF16)
         grad_depth = normalise_grad(hat, scale, dot(grad_act, expand_w[k], NT))
         copies = halo_send(2 + k, grad_depth)
+        if k == 0:
+            stage_second("A")
         put_tall(name, hidden, cotangent)
         put_wide(name, normed, grad_act)
         begin(name)
         pad_inner(2 + k, grad_depth)
         kernel_grad(k, grad_depth)
+        stage_first(name)
         if k == 0:
-            stage_second("A")
-        stage_first(name)
+            stage_third("A")
         halo_wait(2 + k, copies)
         cotangent = (cotangent.astype(F32) + convolve(2 + k, taps_of(k), True)).astype(BF16)
-    stage_third("A")
     stage_second("B")
 
     parts = []
@@ -643,8 +644,8 @@
         s["Cgq"][h, 41:48] = jnp.zeros((7, 16, 128), BF16)
     begin("C")
     stage_first("C")
+    stage_gather("A")
     stage_third("B")
-    stage_gather("A")
     stage_second("C")
     stage_back_second("A")
     stage_gather("B")

time: 93.9 us -> 94.8 us (level)
  no operation moved by 1% of the time
where the time goes in v6:
time: 94.8 us; the launch traced here: 94.7 us
  Pallas kernels  93.9 us (99%)
    pallas_call x1, Pallas kernels, on_device(): pl.pallas_call(functools.partial(net_kernel, nx, ny, nz, tuple(plan)), ou...  91.4 us
    pallas_call x1, Pallas kernels, on_device(): pl.pallas_call(widen_kernel, out_shape=shapes, in_specs=[vmem] * 7, out_s...  2.5 us

profile of v6, /device:TPU:1, one launch (start us, length us, event | category | flops | bytes accessed | tf_op | source)
XLA Modules:
  0.0 94.7 jit_solution(2112632720814094196)
XLA Ops:
  0.6 91.4 %shard_map.145 = (bf16[64,256]{1,0:T(8,128)(2,1)S(1)}, bf16[2,64,16,128]{3,2,1,0:T(8,128)(2,1)S(1)}, bf16[2,64,16,128]{3,2,1,0:T(8,128)(2,1)S(1)}, bf16[2,64,16,...) custom-call(s32[1,64]{1,0:T(1,128)} %bitcast.12, ...), custom_call_target="tpu_custom_call" | custom-call | tf_op jit(solution)/shard_map/pallas_call | solution.py:728
  92.1 2.5 %shard_map.146 = (bf16[64,256]{1,0:T(8,128)(2,1)}, f32[17,256]{1,0:T(8,128)}, f32[1024,256]{1,0:T(8,128)}, f32[49,2,256]{2,1,0:T(2,128)}, f32[2,256,1024]{2,1,0:T(8,128)}, /*index=5*/f32[2,1024,256]{2,1,0:T(8,128)}) custom-call(bf16[64,256]{1,0:T(8,128)(2,1)S(1)} %get-tuple-element.19.feat, bf16[2,64,16,128]{3,2,1,0:T(8,128)(2,1)S(1)} %get-tuple-element.20.afp, ...), custom_call_target="tpu_custom_call" | custom-call | tf_op jit(solution)/shard_map/pallas_call | solution.py:748
